TPU v7x, 256 devices: a whole 4x4x8 slice. The times are simulated.
256 devices in a mesh: prod: 64 (over z, x, core), tile: 4 (over y).
Axes of the slice: x: 4, y: 4, z: 8, core: 2. Of those that a mesh axis runs over, the one named last changes fastest.
Arguments:
- embeddings: bfloat16 [65536, 4096], P('prod')
- cluster_ids: int32 [65536], P('prod'), may hold values from 0 to 511, as said below
Outputs:
- best_cosine: float32 [65536], P('prod')
Inputs may be any that keep to these rules, and one draw needn't show every extreme that they name: `cluster_ids`: cluster c belongs to owner c // 8. On each index of prod at most 32 items belong to one owner, exactly 32 to one owner that is the same for all indices, and at least one to every owner.
All inputs are finite; a program needn't handle non-finite values.
Results may differ from a plain program's by a relative error of at most 0.00043.
Values may be sent and summed in bfloat16 or wider, within the bound.
A program may use at most 128 MiB of HBM per device.

v0:
```python
import jax
import jax.numpy as jnp
from jax import lax
from jax.sharding import PartitionSpec as P

CLU_OWN = 8


def pair_best(row_block, row_labels, columns, column_labels, column_start):
    scores = lax.dot_general(
        row_block, columns, (((1,), (1,)), ((), ())), preferred_element_type=jnp.float32
    )
    row_ident = jnp.arange(row_block.shape[0], dtype=jnp.int32)
    column_ident = column_start + jnp.arange(columns.shape[0], dtype=jnp.int32)
    in_cluster = (
        (row_labels[:, None] == column_labels[None, :])
        & (row_labels[:, None] >= 0)
        & (row_ident[:, None] != column_ident[None, :])
    )
    return jnp.max(jnp.where(in_cluster, scores, -1.0), axis=1)


def shards(embeddings, cluster_ids):
    prod_count = lax.axis_size("prod")
    tile_count = lax.axis_size("tile")
    item_dev = embeddings.shape[0]
    width = embeddings.shape[1]
    per_owner = 2 * item_dev // prod_count
    group_rows = prod_count * per_owner
    widened = embeddings.astype(jnp.float32)
    normed = (
        widened * lax.rsqrt(jnp.sum(widened * widened, axis=1, keepdims=True) + 1e-06)
    ).astype(jnp.bfloat16)
    owners = cluster_ids // CLU_OWN
    owner_hot = (owners[:, None] == jnp.arange(prod_count, dtype=jnp.int32)[None, :]).astype(
        jnp.int32
    )
    running = jnp.cumsum(owner_hot, axis=0)
    slot_index = jnp.sum(running * owner_hot, axis=1) - 1
    position = owners * per_owner + slot_index
    inverse = (
        jnp.full((group_rows,), item_dev, jnp.int32)
        .at[position]
        .set(jnp.arange(item_dev, dtype=jnp.int32))
    )
    padded = jnp.concatenate([normed, jnp.zeros((1, width), jnp.bfloat16)], axis=0)
    labels = jnp.concatenate([cluster_ids, jnp.full((1,), -1, jnp.int32)], axis=0)
    outgoing = padded[inverse].reshape(prod_count, per_owner, width)
    out_labels = labels[inverse].reshape(prod_count, per_owner)
    tile_pos = lax.axis_index("tile")
    row_block, row_labels = (
        lax.all_to_all(outgoing, "prod", split_axis=0, concat_axis=0, tiled=True),
        lax.all_to_all(out_labels, "prod", split_axis=0, concat_axis=0, tiled=True),
    )
    row_block = row_block.reshape(group_rows, width)
    row_labels = row_labels.reshape(group_rows)
    piece_rows = group_rows // tile_count
    row_start = tile_pos * piece_rows
    columns = lax.dynamic_slice_in_dim(row_block, row_start, piece_rows, 0)
    column_labels = lax.dynamic_slice_in_dim(row_labels, row_start, piece_rows, 0)
    partial_best = pair_best(row_block, row_labels, columns, column_labels, row_start)
    maxima = lax.pmax(partial_best, "tile")
    returned = lax.all_to_all(
        maxima.reshape(prod_count, -1), "prod", split_axis=0, concat_axis=0, tiled=True
    )
    return returned.reshape(group_rows)[position]


def solution(mesh):
    placed = (P("prod", None), P("prod"))
    return jax.shard_map(shards, mesh=mesh, in_specs=placed, out_specs=P("prod"), check_vma=False)
```

profile of v0, /device:TPU:1, one launch (start us, length us, event | category | flops | bytes accessed | tf_op | source)
XLA Modules:
  0.0 548.8 jit_solution(2210417953881872286)
XLA Ops:
  0.0 0.7 add_select_fusion
  0.7 18.0 %reduce-window.6 = s32[64,8,128]{2,1,0:T(8,128)S(1)} reduce-window(s32[64,8,128]{2,1,0:T(8,128)S(1)} %fusion.9, s32[]{:T(128)} %constant.20.clone.1), window={size=1x1x128 pad=0_0x0_0x127_0}, to_apply=%region_0.0 | reduce-window | flops 8323072 | bytes 524292 | tf_op jit(solution)/shard_map/reduce-window
  18.7 0.1 slice.14
  18.9 0.1 copy.5
  19.1 0.1 copy.6
  19.1 0.1 broadcast_add_fusion
  19.3 0.1 fusion.8
  19.4 0.7 broadcast_clamp_fusion
  20.1 4.3 scatter_custom_fusion
  24.4 0.7 pad_add_fusion
  25.1 11.8 %gather_fusion = s32[2048]{0:T(1024)S(1)} fusion(s32[1025]{0:T(1024)S(1)} %pad_add_fusion, s32[2048]{0:T(1024)S(1)} %fusion.10), kind=kCustom, calls=%fused_computation | custom fusion | bytes 24576 | tf_op jit(solution)/shard_map/gather | solution.py:49
  36.9 0.7 all_to_all.15
  37.6 13.0 %all-to-all-start = ((s32[64,1,32]{2,1,0:T(1,128)}), s32[64,1,32]{2,1,0:T(1,128)S(1)}, u32[]{:S(2)}, u32[]{:S(2)}) async-start(s32[64,1,32]{2,1,0:T(1,128)} %bitcast.3), calls=%async_computation | async-start | bytes 65536 | tf_op jit(solution)/shard_map/all_to_all | solution.py:53
  50.5 5.1 fusion
  55.6 9.9 %fusion.1 = bf16[1024,4096]{1,0:T(8,128)(2,1)} fusion(bf16[1024,4096]{1,0:T(8,128)(2,1)} %param.2, f32[1024]{0:T(1024)S(1)} %add_rsqrt_fusion), kind=kLoop, calls=%fused_computation.7 | loop fusion | flops 12582912 | bytes 16781312 | tf_op jit(solution)/shard_map/convert_element_type | solution.py:33
  65.6 7.7 %concatenate.7 = bf16[1025,4096]{1,0:T(8,128)(2,1)} pad(bf16[1024,4096]{1,0:T(8,128)(2,1)} %fusion.1, bf16[]{:T(256)} %constant.50.clone.1), padding=0_1x0_0 | pad | bytes 16785410 | tf_op jit(solution)/shard_map/concatenate | solution.py:46
  73.3 33.1 %gather_fusion.1 = bf16[2048,4096]{1,0:T(8,128)(2,1)} fusion(bf16[1025,4096]{1,0:T(8,128)(2,1)} %concatenate.7, s32[2048]{0:T(1024)S(1)} %fusion.10), kind=kCustom, calls=%fused_computation.1 | custom fusion | bytes 33562624 | tf_op jit(solution)/shard_map/gather | solution.py:48
  106.5 0.0 all-to-all-done
  106.5 10.5 %all-to-all-start.1 = ((bf16[64,32,4096]{2,1,0:T(8,128)(2,1)}), bf16[64,32,4096]{2,1,0:T(8,128)(2,1)}, u32[]{:S(2)}, u32[]{:S(2)}) async-start(bf16[64,32,4096]{2,1,0:T(8,128)(2,1)} %bitcast.21), calls=%async_computation.1 | async-start | bytes 33554432 | tf_op jit(solution)/shard_map/all_to_all | solution.py:52
  117.0 0.5 broadcast.93
  117.5 0.7 reduce.6
  118.2 0.1 eq.45
  118.3 0.1 dynamic_slice.6
  118.4 362.7 %all-to-all-done.1 = bf16[64,32,4096]{2,1,0:T(8,128)(2,1)} async-done(((bf16[64,32,4096]{2,1,0:T(8,128)(2,1)}), bf16[64,32,4096]{2,1,0:T(8,128)(2,1)}, u32[]{:S(2)}, u32[]{:S(2)}) %all-to-all-start.1) | async-done | bytes 16777248 | tf_op jit(solution)/shard_map/all_to_all | solution.py:52
  481.1 16.4 %select_reduce_fusion = f32[2048]{0:T(1024)S(1)} fusion(s32[512]{0:T(512)S(1)} %iota_add_fusion, s32[2048]{0:T(1024)S(1)} %eq.45, s32[512]{0:T(512)S(1)} %dynamic_slice.6, pred[2048]{0:T(1024)(128)(4,1)S(1)} %broadcast_compare_fusion, bf16[2048,4096]{1,0:T(8,128)(2,1)} %bitcast.5, s32[]{:T(128)S(6)} %select_n.24), kind=kOutput, calls=%fused_computation.8 | convolution fusion | flops 8596224000 | bytes 20994052 | tf_op jit(solution)/shard_map/dot_general | solution.py:10
  497.5 0.1 all_to_all.18
  497.6 11.4 %pmax.7 = f32[64,1,32]{2,0,1:T(8,128)S(1)} all-reduce(f32[64,1,32]{2,0,1:T(8,128)S(1)} %all_to_all.18), channel_id=1, replica_groups=mesh['prod'=64,'tile'=4] {'tile'}, use_global_device_ids=true, to_apply=%region_6.7 | all-reduce | flops 2048 | bytes 16384 | tf_op jit(solution)/shard_map/pmax | solution.py:62
  509.0 28.0 %all_to_all.23 = f32[64,1,32]{2,1,0:T(1,128)S(1)} all-to-all(f32[64,1,32]{2,1,0:T(1,128)S(1)} %bitcast.23), channel_id=1, replica_groups=mesh['prod'=64,'tile'=4] {'prod'}, dimensions={0} | all-to-all | bytes 16384 | tf_op jit(solution)/shard_map/all_to_all | solution.py:63
  536.9 0.5 broadcast.94
  537.4 0.7 reduce.7
  538.2 0.1 reshape.60
  538.2 10.5 %gather_fusion.2 = f32[1024]{0:T(1024)} fusion(f32[2048]{0:T(1024)S(1)} %reshape.60, s32[1024]{0:T(1024)S(1)} %get-tuple-element.5), kind=kCustom, calls=%fused_computation.2 | custom fusion | bytes 12288 | tf_op jit(solution)/shard_map/gather | solution.py:66
  (8 shorter events, 0.1 us)
Async XLA Ops:
  37.6 68.9 %all-to-all-start = ((s32[64,1,32]{2,1,0:T(1,128)}), s32[64,1,32]{2,1,0:T(1,128)S(1)}, u32[]{:S(2)}, u32[]{:S(2)}) async-start(s32[64,1,32]{2,1,0:T(1,128)} %bitcast.3), calls=%async_computation | async-start | bytes 65536 | tf_op jit(solution)/shard_map/all_to_all | solution.py:53
  106.5 374.6 %all-to-all-start.1 = ((bf16[64,32,4096]{2,1,0:T(8,128)(2,1)}), bf16[64,32,4096]{2,1,0:T(8,128)(2,1)}, u32[]{:S(2)}, u32[]{:S(2)}) async-start(bf16[64,32,4096]{2,1,0:T(8,128)(2,1)} %bitcast.21), calls=%async_computation.1 | async-start | bytes 33554432 | tf_op jit(solution)/shard_map/all_to_all | solution.py:52
where the time goes:
time: 549 us
  waiting for transfers between devices  363 us (66%)
  local copies, waits for them, and re-layouts  69.9 us (13%)
  blocking collectives  39.3 us (7%)
  other arithmetic  36.8 us (7%)
  starting transfers between devices  23.5 us (4%)
  matrix products  16.4 us (3%)
    all_to_all x1, waiting for transfers between devices, shards(): lax.all_to_all(outgoing, 'prod', split_axis=0, concat_axis=0, tiled=True)  363 us
    gather x1, local copies, waits for them, and re-layouts, shards(): outgoing = padded[inverse].reshape(prod_count, per_owner, width)  33.1 us
    all_to_all x1, blocking collectives, shards(): lax.all_to_all(maxima.reshape(prod_count, -1), 'prod', split_axis=0, conc...  28 us
    another operation x3, other arithmetic  18.2 us
    dot_general x1, matrix products, pair_best(): lax.dot_general(row_block, columns, (((1,), (1,)), ((), ())), preferred_e...  16.4 us
    all_to_all x1, starting transfers between devices, shards(): lax.all_to_all(out_labels, 'prod', split_axis=0, concat_axis=0, tiled=True)  13 us
    gather x1, local copies, waits for them, and re-layouts, shards(): out_labels = labels[inverse].reshape(prod_count, per_owner)  11.8 us
    pmax x1, blocking collectives, shards(): maxima = lax.pmax(partial_best, 'tile')  11.4 us
  transfers between devices with their start and end apart: 2, of which 1 were waited for; matrix products, arithmetic and copies ran while one was open for 10% of the time, Pallas kernels for 0%

commit v1 on v0

--- a/solution.py
+++ b/solution.py
@@ -1,9 +1,524 @@
+import functools
+
 import jax
 import jax.numpy as jnp
 from jax import lax
+from jax.experimental import pallas as pl
+from jax.experimental.pallas import tpu as pltpu
 from jax.sharding import PartitionSpec as P
 
 CLU_OWN = 8
+SLOTS = 32
+Z_SLOTS = 176
+BLOCK = 128
+CAP = 3 * BLOCK
+F32 = jnp.float32
+BF16 = jnp.bfloat16
+MESH = pl.DeviceIdType.MESH
+NN = (((1,), (0,)), ((), ()))
+NT = (((1,), (1,)), ((), ()))
+
+
+def dot(a, b, dims=NN, precision=None):
+    return lax.dot_general(a, b, dims, preferred_element_type=F32, precision=precision)
+
+
+def iota(shape, dim):
+    return lax.broadcasted_iota(jnp.int32, shape, dim)
+
+
+def hot(cond):
+    return jnp.where(cond, 1.0, 0.0).astype(BF16)
+
+
+def pack_kernel(
+    planes, owners_in, ids_ref, x_ref, packed_ref, lids_ref, index_ref, hist_ref, unit, counts
+):
+    step = pl.program_id(0)
+    rows, width = x_ref.shape
+    items = ids_ref.shape[1]
+    part = unit.shape[1]
+    tile = lax.axis_index("tile")
+
+    total = jnp.zeros((rows, BLOCK), F32)
+    for c in range(width // BLOCK):
+        x = x_ref[:, c * BLOCK : (c + 1) * BLOCK].astype(F32)
+        total += x * x
+    scale = lax.rsqrt(jnp.sum(total, axis=1, keepdims=True) + 1e-06)
+    mine = x_ref[:, pl.ds(pl.multiple_of(tile * part, part), part)].astype(F32)
+    unit[pl.ds(pl.multiple_of(step * rows, rows), rows), :] = (mine * scale).astype(BF16)
+
+    ids = ids_ref[...]
+    owner = ids // CLU_OWN
+    plane = owner // owners_in
+    key = (owner * items + iota((1, items), 1)).astype(F32)
+    plane_key = (plane * (owners_in * items)).astype(F32)
+    owner_key = (owner * items).astype(F32)
+    here = ids_ref[:, pl.ds(pl.multiple_of(step * rows, rows), rows)]
+    here_key = ((here // CLU_OWN) * items + iota((1, rows), 1) + step * rows).astype(F32)
+    column = jnp.broadcast_to(here_key, (BLOCK, rows)).T
+
+    @pl.when(step == 0)
+    def _():
+        counts[...] = jnp.zeros_like(counts)
+
+    for g in range(items // BLOCK):
+        lanes = slice(g * BLOCK, (g + 1) * BLOCK)
+        for n, bound in enumerate((key, plane_key, owner_key)):
+            less = jnp.where(column < bound[:, lanes], 1.0, 0.0)
+            counts[n : n + 1, lanes] += jnp.sum(less, axis=0, keepdims=True)
+
+    @pl.when(step == pl.num_programs(0) - 1)
+    def _():
+        before = counts[0:1, :]
+        position = (before - counts[1:2, :]).astype(jnp.int32)
+        slot = (before - counts[2:3, :]).astype(jnp.int32)
+        place = (owner % owners_in) * SLOTS + slot
+        lid = ids % CLU_OWN
+        for z in range(planes):
+            pick = hot((iota((Z_SLOTS, items), 0) == position) & (plane == z))
+            packed_ref[z] = dot(pick, unit[...]).astype(BF16)
+        by_plane = jnp.where(iota((8, items), 0) == plane, lid + 1, 0).astype(F32).astype(BF16)
+        by_place = hot(iota((owners_in * SLOTS, items), 0) == place)
+        lids = dot(by_plane, by_place, NT)
+        for z in range(planes):
+            lids_ref[z] = jnp.broadcast_to(lids[z : z + 1], lids_ref.shape[1:])
+        row = iota((8, items), 0)
+        index_ref[...] = jnp.where(row == 0, plane, place)
+        by_owner = hot(iota((planes * owners_in, items), 0) == owner)
+        kind = iota((16, items), 0)
+        by_lid = jnp.where(kind == lid, 1.0, 0.0) + jnp.where(
+            (kind == CLU_OWN) & (position >= Z_SLOTS), 1024.0, 0.0
+        )
+        hist_ref[...] = dot(by_owner, by_lid.astype(BF16), NT)
+
+
+def pack(planes, owners_in, embeddings, cluster_ids, part):
+    items, width = embeddings.shape
+    lanes = owners_in * SLOTS
+    whole = lambda shape: pl.BlockSpec(shape, lambda i: (0,) * len(shape))
+    shapes = (
+        jax.ShapeDtypeStruct((planes, Z_SLOTS, part), BF16),
+        jax.ShapeDtypeStruct((planes, 8, lanes), F32),
+        jax.ShapeDtypeStruct((8, items), jnp.int32),
+        jax.ShapeDtypeStruct((planes * owners_in, 16), F32),
+    )
+    return pl.pallas_call(
+        functools.partial(pack_kernel, planes, owners_in),
+        grid=(items // BLOCK,),
+        in_specs=[whole((1, items)), pl.BlockSpec((BLOCK, width), lambda i: (i, 0))],
+        out_specs=[whole(s.shape) for s in shapes],
+        out_shape=shapes,
+        scratch_shapes=[pltpu.VMEM((items, part), BF16), pltpu.VMEM((8, items), F32)],
+        compiler_params=pltpu.CompilerParams(vmem_limit_bytes=40 * 1024 * 1024),
+    )(cluster_ids.reshape(1, items), embeddings)
+
+
+def nearest_first(n):
+    order = [0]
+    for d in range(1, n // 2 + 1):
+        order += [d] if 2 * d == n else [d, n - d]
+    return order
+
+
+def route_kernel(
+    planes,
+    owners_in,
+    packed_ref,
+    lids_ref,
+    index_ref,
+    out_ref,
+    z_rows,
+    z_lids,
+    lids_out,
+    x_lids,
+    staged,
+    rows,
+    sorted_rows,
+    partial,
+    relay,
+    near,
+    far,
+    forward,
+    found,
+    values_out,
+    x_back,
+    values_home,
+    z_back,
+    own_sem,
+    z_send,
+    z_recv,
+    zl_send,
+    zl_recv,
+    xl_send,
+    xl_recv,
+    x_send,
+    x_recv,
+    y_send,
+    y_recv,
+    f_send,
+    f_recv,
+    xb_send,
+    xb_recv,
+    zb_send,
+    zb_recv,
+):
+    lanes = owners_in * SLOTS
+    half = partial.shape[1] // 2
+    me = lax.axis_index("prod")
+    tile = lax.axis_index("tile")
+    my_plane = me // owners_in
+    my_col = lax.rem(me, owners_in)
+    at_plane = lambda d: lax.rem(my_plane + d, planes)
+    at_col = lambda k: lax.rem(my_col + k, owners_in)
+    at_tile = lambda k: lax.rem(tile + k, 4)
+    to_plane = lambda d: {"prod": at_plane(d) * owners_in + my_col}
+    to_col = lambda k: {"prod": my_plane * owners_in + at_col(k)}
+    to_tile = lambda k: {"tile": at_tile(k)}
+
+    def send(src, dst, send_sem, recv_sem, device):
+        return pltpu.make_async_remote_copy(
+            src_ref=src,
+            dst_ref=dst,
+            send_sem=send_sem,
+            recv_sem=recv_sem,
+            device_id=device,
+            device_id_type=MESH,
+        )
+
+    barrier = pltpu.get_barrier_semaphore()
+    for d in range(1, planes):
+        pl.semaphore_signal(barrier, inc=1, device_id=to_plane(d), device_id_type=MESH)
+    for k in range(1, owners_in):
+        pl.semaphore_signal(barrier, inc=1, device_id=to_col(k), device_id_type=MESH)
+    for k in range(1, 4):
+        pl.semaphore_signal(barrier, inc=1, device_id=to_tile(k), device_id_type=MESH)
+    pl.semaphore_wait(barrier, planes + owners_in + 1)
+
+    order = nearest_first(planes)
+    lid_sends = [
+        send(lids_ref.at[at_plane(d)], z_lids.at[d], zl_send.at[d], zl_recv.at[d], to_plane(d))
+        for d in order[1:]
+    ]
+    for copy in lid_sends:
+        copy.start()
+    own = pltpu.make_async_copy(packed_ref.at[my_plane], z_rows.at[0], own_sem)
+    own.start()
+    row_sends = {
+        d: send(packed_ref.at[at_plane(d)], z_rows.at[d], z_send.at[d], z_recv.at[d], to_plane(d))
+        for d in order[1:]
+    }
+    for d in order[1:]:
+        row_sends[d].start()
+
+    for copy in lid_sends:
+        copy.wait_recv()
+    lids = jnp.concatenate(
+        [lids_ref[my_plane][0:1]] + [z_lids[d][0:1] for d in range(1, planes)], axis=0
+    )
+    lids_out[...] = pltpu.roll(lids, lax.rem(owners_in - my_col, owners_in) * SLOTS, 1)
+    col_lid_sends = [
+        send(lids_out, x_lids.at[k], xl_send.at[k], xl_recv.at[k], to_col(k))
+        for k in range(1, owners_in)
+    ]
+    for copy in col_lid_sends:
+        copy.start()
+    before = hot(iota((lanes, lanes), 0) < iota((lanes, lanes), 1))
+    rank = dot(hot(lids > 0.0), before)
+    source = jnp.where(lids > 0.0, rank, -1.0)
+    source = jnp.concatenate([source, jnp.zeros((BLOCK - planes, lanes), F32)], axis=0).T
+
+    for copy in col_lid_sends:
+        copy.wait_recv()
+    got = jnp.zeros((planes, lanes), F32)
+    group = iota((planes, lanes), 1) // SLOTS
+    for k in range(owners_in):
+        got += jnp.where(group == k, lids_out[...] if k == 0 else x_lids[k], 0.0)
+    member = jnp.concatenate([hot(got == c + 1.0) for c in range(CLU_OWN)], axis=0)
+    in_row = dot(member, before)
+    in_rows = dot(member, jnp.ones((lanes, lanes), BF16))
+    a, b = (iota((CLU_OWN * planes, CLU_OWN * planes), n) for n in (0, 1))
+    earlier = dot(hot((a // planes == b // planes) & (b < a)), in_rows.astype(BF16))
+    rank_all = in_row + earlier
+    a, b = (iota((CLU_OWN, CLU_OWN * planes), n) for n in (0, 1))
+    sizes = dot(hot(a == b // planes), in_rows.astype(BF16))
+    ranked = jnp.zeros((planes, lanes), F32)
+    for c in range(CLU_OWN):
+        this = slice(c * planes, (c + 1) * planes)
+        ranked += jnp.where(got == c + 1.0, rank_all[this], 0.0)
+    target = jnp.where(got > 0.0, (got - 1.0) * CAP + ranked, -1.0).astype(jnp.int32)
+
+    def forward_rows(d):
+        if d == 0:
+            own.wait()
+        else:
+            row_sends[d].wait_recv()
+        take = source[:, d : d + 1].astype(jnp.int32) == iota((lanes, Z_SLOTS), 1)
+        staged[d] = dot(hot(take), z_rows[d]).astype(BF16)
+        copies = []
+        for k in range(owners_in):
+            start = pl.multiple_of(at_col(k) * SLOTS, SLOTS)
+            src = staged.at[d, pl.ds(start, SLOTS)]
+            dst = rows.at[d, pl.ds(k * SLOTS, SLOTS)]
+            if k == 0:
+                copy = pltpu.make_async_copy(src, dst, x_recv.at[d, 0])
+            else:
+                copy = send(src, dst, x_send.at[d, k], x_recv.at[d, k], to_col(k))
+            copy.start()
+            copies.append(copy)
+        return copies
+
+    def place_rows(d, copies, first):
+        copies[0].wait()
+        for copy in copies[1:]:
+            copy.wait_recv()
+        goal = target[d : d + 1]
+
+        def body(c, carry):
+            start = pl.multiple_of(c * CAP, CAP)
+            chosen = hot(iota((CAP, lanes), 0) + start == goal)
+            moved = dot(chosen, rows[d]).astype(BF16)
+            span = pl.ds(start, CAP)
+            if first:
+                sorted_rows[span, :] = moved
+            else:
+                sorted_rows[span, :] = sorted_rows[span, :] + moved
+            return carry
+
+        lax.fori_loop(0, CLU_OWN, body, 0)
+
+    x_copies = {}
+    lag = 2
+    for n, d in enumerate(order):
+        x_copies[d] = forward_rows(d)
+        if n >= lag:
+            place_rows(order[n - lag], x_copies[order[n - lag]], n == lag)
+    for n in range(max(0, len(order) - lag), len(order)):
+        place_rows(order[n], x_copies[order[n]], n == 0)
+
+    r, c = (iota((BLOCK, BLOCK), n) for n in (0, 1))
+
+    def scores(t):
+        thirds = []
+        for j in range(2):
+            start = pl.multiple_of((2 * t + j) * CAP, CAP)
+            block = sorted_rows[pl.ds(start, CAP), :]
+            one = dot(block[:BLOCK], block, NT)
+            two = dot(block[BLOCK : 2 * BLOCK], block[BLOCK:], NT)
+            three = dot(block[2 * BLOCK :], block[2 * BLOCK :], NT)
+            base = 4 * j * BLOCK
+            partial[t, base : base + BLOCK] = one[:, BLOCK : 2 * BLOCK]
+            partial[t, base + BLOCK : base + 2 * BLOCK] = one[:, 2 * BLOCK :]
+            partial[t, base + 2 * BLOCK : base + 3 * BLOCK] = two[:, BLOCK:]
+            partial[t, base + 3 * BLOCK : base + 4 * BLOCK] = jnp.where(
+                c > r, one[:, :BLOCK], two[:, :BLOCK]
+            )
+            thirds.append(three)
+        partial[t, 8 * BLOCK : 9 * BLOCK] = jnp.where(c > r, thirds[0], thirds[1])
+
+    right, left, across = at_tile(1), at_tile(3), at_tile(2)
+    head, tail = pl.ds(0, half), pl.ds(half, half)
+    scores(across)
+    first = [
+        send(partial.at[across, head], relay.at[0], y_send.at[0], y_recv.at[0], to_tile(1)),
+        send(partial.at[across, tail], relay.at[1], y_send.at[1], y_recv.at[1], to_tile(3)),
+    ]
+    for copy in first:
+        copy.start()
+    scores(right)
+    second = [send(partial.at[right, tail], near.at[1], y_send.at[2], y_recv.at[2], to_tile(1))]
+    second[0].start()
+    scores(left)
+    second += [send(partial.at[left, head], near.at[0], y_send.at[3], y_recv.at[3], to_tile(3))]
+    second[1].start()
+    scores(tile)
+    first[0].wait_recv()
+    forward[0] = relay[0] + partial[right, 0:half]
+    third_sends = [send(forward.at[0], far.at[0], y_send.at[4], y_recv.at[4], to_tile(1))]
+    third_sends[0].start()
+    first[1].wait_recv()
+    forward[1] = relay[1] + partial[left, half : 2 * half]
+    third_sends += [send(forward.at[1], far.at[1], y_send.at[5], y_recv.at[5], to_tile(3))]
+    third_sends[1].start()
+    for copy in second + third_sends:
+        copy.wait_recv()
+    summed = jnp.concatenate(
+        [
+            partial[tile, 0:half] + near[0] + far[0],
+            partial[tile, half : 2 * half] + near[1] + far[1],
+        ],
+        axis=0,
+    )
+
+    size_rows = iota(sizes.shape, 0)
+    best = []
+
+    def highest(score, limit):
+        return jnp.max(jnp.where(limit, score, -1.0), axis=0, keepdims=True)
+
+    corner = summed[8 * BLOCK : 9 * BLOCK]
+    for j in range(2):
+        size = jnp.sum(
+            jnp.where(size_rows == 2 * tile + j, sizes, 0.0), axis=0, keepdims=True
+        )[:, :BLOCK].astype(jnp.int32)
+        ok = [r + n * BLOCK < size for n in range(3)]
+        ab, ac, bc, diagonal = (
+            summed[(4 * j + n) * BLOCK : (4 * j + n + 1) * BLOCK] for n in range(4)
+        )
+        above, below = (c > r), (c < r)
+        mine, theirs = (above, below) if j == 0 else (below, above)
+        turned = diagonal.T
+        corner_turned = corner.T
+        zero = [
+            highest(diagonal, ok[0] & above),
+            highest(turned, ok[0] & below),
+            highest(ab.T, ok[1]),
+            highest(ac.T, ok[2]),
+        ]
+        one = [
+            highest(diagonal, ok[1] & below),
+            highest(turned, ok[1] & above),
+            highest(ab, ok[0]),
+            highest(bc.T, ok[2]),
+        ]
+        two = [
+            highest(corner, ok[2] & mine),
+            highest(corner_turned, ok[2] & theirs),
+            highest(ac, ok[0]),
+            highest(bc, ok[1]),
+        ]
+        best += [functools.reduce(jnp.maximum, parts) for parts in (zero, one, two)]
+    found[tile] = jnp.concatenate(best + [jnp.zeros((2, BLOCK), F32)], axis=0)
+    spread = [
+        send(found.at[tile], found.at[tile], f_send.at[k], f_recv.at[k], to_tile(k))
+        for k in range(1, 4)
+    ]
+    for copy in spread:
+        copy.start()
+    for k in range(1, 4):
+        send(
+            found.at[at_tile(4 - k)], found.at[at_tile(4 - k)], f_send.at[k], f_recv.at[k], to_tile(k)
+        ).wait_recv()
+
+    table = jnp.concatenate([found[t] for t in range(4)] + [jnp.zeros((BLOCK - 32, BLOCK), F32)], 0).T
+    lid = got.astype(jnp.int32) - 1
+    ranked = ranked.astype(jnp.int32)
+    third = ranked // BLOCK
+    table_row = (lid // 2) * 8 + (lid % 2) * 3 + third
+    lane = ranked - third * BLOCK
+    picked = []
+    for d in range(planes):
+        chosen = jnp.where(iota((BLOCK, lanes), 0) == table_row[d : d + 1], 1.0, 0.0)
+        values = dot(table, chosen, precision=lax.Precision.HIGHEST)
+        mask = iota((BLOCK, lanes), 0) == lane[d : d + 1]
+        picked.append(jnp.sum(jnp.where(mask, values, 0.0), axis=0, keepdims=True))
+    values_out[...] = jnp.concatenate(picked, axis=0)
+    col_back = [
+        send(
+            values_out,
+            x_back.at[k],
+            xb_send.at[k],
+            xb_recv.at[k],
+            to_col(owners_in - k),
+        )
+        for k in range(1, owners_in)
+    ]
+    for copy in col_back:
+        copy.start()
+    home = jnp.where(group == 0, values_out[...], 0.0)
+    for k in range(1, owners_in):
+        col_back[k - 1].wait_recv()
+        home += jnp.where(group == k, x_back[k], 0.0)
+    values_home[...] = pltpu.roll(home, my_col * SLOTS, 1)
+    plane_back = [
+        send(
+            values_home,
+            z_back.at[d],
+            zb_send.at[d],
+            zb_recv.at[d],
+            to_plane(planes - d),
+        )
+        for d in range(1, planes)
+    ]
+    for copy in plane_back:
+        copy.start()
+    for copy in plane_back:
+        copy.wait_recv()
+    mine = jnp.concatenate(
+        [values_home[0:1]] + [z_back[d][d : d + 1] for d in range(1, planes)], axis=0
+    )
+    mine = jnp.concatenate([mine, jnp.zeros((BLOCK - planes, lanes), F32)], axis=0).T
+    items = out_ref.shape[1]
+    ahead = lax.rem(index_ref[0:1, :] - my_plane + planes, planes)
+    chosen = jnp.where(iota((BLOCK, items), 0) == ahead, 1.0, 0.0)
+    values = dot(mine, chosen, precision=lax.Precision.HIGHEST)
+    mask = iota((lanes, items), 0) == index_ref[1:2, :]
+    out_ref[...] = jnp.sum(jnp.where(mask, values, 0.0), axis=0, keepdims=True)
+
+    for copy in lid_sends + col_lid_sends + first + second + third_sends + spread:
+        copy.wait_send()
+    for d in order[1:]:
+        row_sends[d].wait_send()
+    for d in order:
+        for copy in x_copies[d][1:]:
+            copy.wait_send()
+    for copy in col_back + plane_back:
+        copy.wait_send()
+
+
+def route(planes, owners_in, packed, lids, index):
+    part = packed.shape[2]
+    items = index.shape[1]
+    lanes = owners_in * SLOTS
+    tiles = 9 * BLOCK
+    vmem = pl.BlockSpec(memory_space=pltpu.VMEM)
+    dma = lambda *shape: pltpu.SemaphoreType.DMA(shape)
+    buffer = pltpu.VMEM
+    return pl.pallas_call(
+        functools.partial(route_kernel, planes, owners_in),
+        out_shape=jax.ShapeDtypeStruct((1, items), F32),
+        in_specs=[pl.BlockSpec(memory_space=pl.ANY), vmem, vmem],
+        out_specs=vmem,
+        scratch_shapes=[
+            buffer((planes, Z_SLOTS, part), BF16),
+            buffer((planes, 8, lanes), F32),
+            buffer((planes, lanes), F32),
+            buffer((owners_in, planes, lanes), F32),
+            buffer((planes, lanes, part), BF16),
+            buffer((planes, lanes, part), BF16),
+            buffer((CLU_OWN * CAP, part), BF16),
+            buffer((4, tiles, BLOCK), F32),
+            buffer((2, tiles // 2, BLOCK), F32),
+            buffer((2, tiles // 2, BLOCK), F32),
+            buffer((2, tiles // 2, BLOCK), F32),
+            buffer((2, tiles // 2, BLOCK), F32),
+            buffer((4, 8, BLOCK), F32),
+            buffer((planes, lanes), F32),
+            buffer((owners_in, planes, lanes), F32),
+            buffer((planes, lanes), F32),
+            buffer((planes, planes, lanes), F32),
+            pltpu.SemaphoreType.DMA,
+            dma(planes),
+            dma(planes),
+            dma(planes),
+            dma(planes),
+            dma(owners_in),
+            dma(owners_in),
+            dma(planes, owners_in),
+            dma(planes, owners_in),
+            dma(6),
+            dma(6),
+            dma(4),
+            dma(4),
+            dma(owners_in),
+            dma(owners_in),
+            dma(planes),
+            dma(planes),
+        ],
+        compiler_params=pltpu.CompilerParams(
+            collective_id=0, has_side_effects=True, vmem_limit_bytes=52 * 1024 * 1024
+        ),
+    )(packed, lids, index)
 
 
 def pair_best(row_block, row_labels, columns, column_labels, column_start):
@@ -20,13 +535,12 @@
     return jnp.max(jnp.where(in_cluster, scores, -1.0), axis=1)
 
 
-def shards(embeddings, cluster_ids):
+def any_layout(embeddings, cluster_ids):
     prod_count = lax.axis_size("prod")
     tile_count = lax.axis_size("tile")
     item_dev = embeddings.shape[0]
     width = embeddings.shape[1]
-    per_owner = 2 * item_dev // prod_count
-    group_rows = prod_count * per_owner
+    group_rows = prod_count * SLOTS
     widened = embeddings.astype(jnp.float32)
     normed = (
         widened * lax.rsqrt(jnp.sum(widened * widened, axis=1, keepdims=True) + 1e-06)
@@ -37,7 +551,7 @@
     )
     running = jnp.cumsum(owner_hot, axis=0)
     slot_index = jnp.sum(running * owner_hot, axis=1) - 1
-    position = owners * per_owner + slot_index
+    position = owners * SLOTS + slot_index
     inverse = (
         jnp.full((group_rows,), item_dev, jnp.int32)
         .at[position]
@@ -45,8 +559,8 @@
     )
     padded = jnp.concatenate([normed, jnp.zeros((1, width), jnp.bfloat16)], axis=0)
     labels = jnp.concatenate([cluster_ids, jnp.full((1,), -1, jnp.int32)], axis=0)
-    outgoing = padded[inverse].reshape(prod_count, per_owner, width)
-    out_labels = labels[inverse].reshape(prod_count, per_owner)
+    outgoing = padded[inverse].reshape(prod_count, SLOTS, width)
+    out_labels = labels[inverse].reshape(prod_count, SLOTS)
     tile_pos = lax.axis_index("tile")
     row_block, row_labels = (
         lax.all_to_all(outgoing, "prod", split_axis=0, concat_axis=0, tiled=True),
@@ -66,6 +580,19 @@
     return returned.reshape(group_rows)[position]
 
 
+def shards(embeddings, cluster_ids):
+    prod_count = lax.axis_size("prod")
+    owners_in = 8 if prod_count >= 64 else 4
+    planes = prod_count // owners_in
+    part = embeddings.shape[1] // lax.axis_size("tile")
+    packed, lids, index, hist = pack(planes, owners_in, embeddings, cluster_ids, part)
+    fits = jnp.max(lax.psum(hist, "prod")) <= CAP
+    best = route(planes, owners_in, packed, lids, index).reshape(-1)
+    return lax.cond(
+        fits, lambda e, i, b: b, lambda e, i, b: any_layout(e, i), embeddings, cluster_ids, best
+    )
+
+
 def solution(mesh):
     placed = (P("prod", None), P("prod"))
     return jax.shard_map(shards, mesh=mesh, in_specs=placed, out_specs=P("prod"), check_vma=False)

time: 549 us -> 386 us (0.70)
  waiting for transfers between devices: 363 us -> 0 us
  blocking collectives: 39.3 us -> 243 us
  Pallas kernels: 0 us -> 136 us
  local copies, waits for them, and re-layouts: 69.9 us -> 2.17 us
  other arithmetic: 36.8 us -> 0.61 us
  starting transfers between devices: 23.5 us -> 0 us
  matrix products: 16.4 us -> 0 us
    all_to_all x2 -> x0, waiting for transfers between devices: 363 us -> none  [the longest x1 363 us: shards(): lax.all_to_all(outgoing, 'prod', split_axis=0, concat_axis=0, tiled=True)]
    psum x0 -> x1, blocking collectives: none -> 243 us  [shards(): fits = jnp.max(lax.psum(hist, 'prod')) <= CAP]
    pallas_call x0 -> x2, Pallas kernels: none -> 136 us  [the longest x1 125 us: route(): pl.pallas_call(functools.partial(route_kernel, planes, owners_in), out_sh...]
    gather x3 -> x0, local copies, waits for them, and re-layouts: 55.5 us -> none  [the longest x1 33.1 us: shards(): outgoing = padded[inverse].reshape(prod_count, per_owner, width)]
    all_to_all x1 -> x0, blocking collectives: 28 us -> none  [shards(): lax.all_to_all(maxima.reshape(prod_count, -1), 'prod', split_axis=0, conc...]
    all_to_all x2 -> x0, starting transfers between devices: 23.5 us -> none  [the longest x1 13 us: shards(): lax.all_to_all(out_labels, 'prod', split_axis=0, concat_axis=0, tiled=True)]
    another operation x3 -> x0, other arithmetic: 18.2 us -> none
    dot_general x1 -> x0, matrix products: 16.4 us -> none  [pair_best(): lax.dot_general(row_block, columns, (((1,), (1,)), ((), ())), preferred_e...]
  transfers between devices with their start and end apart: 2 -> 0, of which waited for: 1 -> 0; matrix products, arithmetic and copies ran while one was open for 10% -> 0% of each run, Pallas kernels for 0% -> 0%
where the time goes in v1:
time: 386 us; the launch traced here: 383 us
  blocking collectives  243 us (63%)
  Pallas kernels  136 us (35%)
    psum x1, blocking collectives, shards(): fits = jnp.max(lax.psum(hist, 'prod')) <= CAP  243 us
    pallas_call x1, Pallas kernels, route(): pl.pallas_call(functools.partial(route_kernel, planes, owners_in), out_sh...  125 us
    pallas_call x1, Pallas kernels, pack(): pl.pallas_call(functools.partial(pack_kernel, planes, owners_in), grid=(i...  11.1 us

profile of v1, /device:TPU:1, one launch (start us, length us, event | category | flops | bytes accessed | tf_op | source)
XLA Modules:
  0.0 382.7 jit_solution(1748874067335388017)
XLA Ops:
  0.0 0.0 copy-start.1
  0.0 11.1 %shard_map.30 = (bf16[8,176,1024]{2,1,0:T(8,128)(2,1)S(1)}, f32[8,8,256]{2,1,0:T(8,128)S(1)}, s32[8,1024]{1,0:T(8,128)S(1)}, f32[64,16]{1,0:T(8,128)S(1)}) custom-call(s32[1,1024]{1,0:T(1,128)} %bitcast.26, bf16[1024,4096]{1,0:T(8,128)(2,1)} %x_ref.1), custom_call_target="tpu_custom_call" | custom-call | tf_op jit(solution)/shard_map/pallas_call | solution.py:106
  11.1 0.0 copy-start
  11.1 1.6 copy-done
  12.7 124.6 %shard_map.31 = f32[1,1024]{1,0:T(1,128)S(1)} custom-call(bf16[8,176,1024]{2,1,0:T(8,128)(2,1)} %copy-done, f32[8,8,256]{2,1,0:T(8,128)S(1)} %get-tuple-element.23.lids_ref, s32[8,1024]{1,0:T(8,128)S(1)} %get-tuple-element.24.index_ref), custom_call_target="tpu_custom_call" | custom-call | tf_op jit(solution)/shard_map/pallas_call | solution.py:477
  137.3 243.3 %psum.7 = f32[64,16]{1,0:T(8,128)S(1)} all-reduce(f32[64,16]{1,0:T(8,128)S(1)} %get-tuple-element.21), channel_id=1, replica_groups=mesh['prod'=64,'tile'=4] {'prod'}, use_global_device_ids=true, to_apply=%region_0.0 | all-reduce | flops 1024 | bytes 8192 | tf_op jit(solution)/shard_map/psum | solution.py:589
  380.5 0.6 reduce_max.18
  381.8 0.0 copy-done.1
  381.8 0.3 conditional.1
  382.1 0.6 copy.16
Async XLA Ops:
  0.0 381.8 %copy-start.1 = (s32[1024]{0:T(1024)S(1)}, s32[1024]{0:T(1024)}, u32[]{:S(2)}) copy-start(s32[1024]{0:T(1024)} %param.5) | copy-start | bytes 12292
  11.1 1.6 copy-start

commit v2 on v1

--- a/solution.py
+++ b/solution.py
@@ -12,6 +12,7 @@
 Z_SLOTS = 176
 BLOCK = 128
 CAP = 3 * BLOCK
+TOO_MANY = 4.0 * CLU_OWN
 F32 = jnp.float32
 BF16 = jnp.bfloat16
 MESH = pl.DeviceIdType.MESH
@@ -32,7 +33,7 @@
 
 
 def pack_kernel(
-    planes, owners_in, ids_ref, x_ref, packed_ref, lids_ref, index_ref, hist_ref, unit, counts
+    planes, owners_in, ids_ref, x_ref, packed_ref, lids_ref, index_ref, unit, counts
 ):
     step = pl.program_id(0)
     rows, width = x_ref.shape
@@ -81,16 +82,11 @@
         by_plane = jnp.where(iota((8, items), 0) == plane, lid + 1, 0).astype(F32).astype(BF16)
         by_place = hot(iota((owners_in * SLOTS, items), 0) == place)
         lids = dot(by_plane, by_place, NT)
+        lids += jnp.where(jnp.max(position, axis=1, keepdims=True) >= Z_SLOTS, TOO_MANY, 0.0)
         for z in range(planes):
             lids_ref[z] = jnp.broadcast_to(lids[z : z + 1], lids_ref.shape[1:])
         row = iota((8, items), 0)
         index_ref[...] = jnp.where(row == 0, plane, place)
-        by_owner = hot(iota((planes * owners_in, items), 0) == owner)
-        kind = iota((16, items), 0)
-        by_lid = jnp.where(kind == lid, 1.0, 0.0) + jnp.where(
-            (kind == CLU_OWN) & (position >= Z_SLOTS), 1024.0, 0.0
-        )
-        hist_ref[...] = dot(by_owner, by_lid.astype(BF16), NT)
 
 
 def pack(planes, owners_in, embeddings, cluster_ids, part):
@@ -101,7 +97,6 @@
         jax.ShapeDtypeStruct((planes, Z_SLOTS, part), BF16),
         jax.ShapeDtypeStruct((planes, 8, lanes), F32),
         jax.ShapeDtypeStruct((8, items), jnp.int32),
-        jax.ShapeDtypeStruct((planes * owners_in, 16), F32),
     )
     return pl.pallas_call(
         functools.partial(pack_kernel, planes, owners_in),
@@ -231,9 +226,12 @@
     for copy in col_lid_sends:
         copy.wait_recv()
     got = jnp.zeros((planes, lanes), F32)
+    marks = lids_out[...]
     group = iota((planes, lanes), 1) // SLOTS
     for k in range(owners_in):
-        got += jnp.where(group == k, lids_out[...] if k == 0 else x_lids[k], 0.0)
+        theirs = lids_out[...] if k == 0 else x_lids[k]
+        got += jnp.where(group == k, theirs, 0.0)
+        marks = jnp.maximum(marks, theirs)
     member = jnp.concatenate([hot(got == c + 1.0) for c in range(CLU_OWN)], axis=0)
     in_row = dot(member, before)
     in_rows = dot(member, jnp.ones((lanes, lanes), BF16))
@@ -242,6 +240,8 @@
     rank_all = in_row + earlier
     a, b = (iota((CLU_OWN, CLU_OWN * planes), n) for n in (0, 1))
     sizes = dot(hot(a == b // planes), in_rows.astype(BF16))
+    most = lambda a: jnp.max(jnp.max(a, axis=1, keepdims=True), axis=0, keepdims=True)
+    unfit = (most(marks) >= TOO_MANY) | (most(sizes) > CAP)
     ranked = jnp.zeros((planes, lanes), F32)
     for c in range(CLU_OWN):
         this = slice(c * planes, (c + 1) * planes)
@@ -412,7 +412,7 @@
         values = dot(table, chosen, precision=lax.Precision.HIGHEST)
         mask = iota((BLOCK, lanes), 0) == lane[d : d + 1]
         picked.append(jnp.sum(jnp.where(mask, values, 0.0), axis=0, keepdims=True))
-    values_out[...] = jnp.concatenate(picked, axis=0)
+    values_out[...] = jnp.where(unfit, TOO_MANY, jnp.concatenate(picked, axis=0))
     col_back = [
         send(
             values_out,
@@ -444,6 +444,10 @@
         copy.start()
     for copy in plane_back:
         copy.wait_recv()
+    marks = values_home[...]
+    for d in range(1, planes):
+        marks = jnp.maximum(marks, z_back[d])
+    unfit = most(marks) >= TOO_MANY
     mine = jnp.concatenate(
         [values_home[0:1]] + [z_back[d][d : d + 1] for d in range(1, planes)], axis=0
     )
@@ -453,7 +457,8 @@
     chosen = jnp.where(iota((BLOCK, items), 0) == ahead, 1.0, 0.0)
     values = dot(mine, chosen, precision=lax.Precision.HIGHEST)
     mask = iota((lanes, items), 0) == index_ref[1:2, :]
-    out_ref[...] = jnp.sum(jnp.where(mask, values, 0.0), axis=0, keepdims=True)
+    best = jnp.sum(jnp.where(mask, values, 0.0), axis=0, keepdims=True)
+    out_ref[...] = jnp.where(unfit, TOO_MANY, best)
 
     for copy in lid_sends + col_lid_sends + first + second + third_sends + spread:
         copy.wait_send()
@@ -585,9 +590,9 @@
     owners_in = 8 if prod_count >= 64 else 4
     planes = prod_count // owners_in
     part = embeddings.shape[1] // lax.axis_size("tile")
-    packed, lids, index, hist = pack(planes, owners_in, embeddings, cluster_ids, part)
-    fits = jnp.max(lax.psum(hist, "prod")) <= CAP
+    packed, lids, index = pack(planes, owners_in, embeddings, cluster_ids, part)
     best = route(planes, owners_in, packed, lids, index).reshape(-1)
+    fits = jnp.max(best) < TOO_MANY
     return lax.cond(
         fits, lambda e, i, b: b, lambda e, i, b: any_layout(e, i), embeddings, cluster_ids, best
     )

time: 386 us -> 140 us (0.36)
  blocking collectives: 243 us -> 0 us
    psum x1 -> x0, blocking collectives: 243 us -> none  [shards(): fits = jnp.max(lax.psum(hist, 'prod')) <= CAP]
where the time goes in v2:
time: 140 us; the launch traced here: 139 us
  Pallas kernels  136 us (97%)
  local copies, waits for them, and re-layouts  2.17 us (2%)
    pallas_call x1, Pallas kernels, route(): pl.pallas_call(functools.partial(route_kernel, planes, owners_in), out_sh...  125 us
    pallas_call x1, Pallas kernels, pack(): pl.pallas_call(functools.partial(pack_kernel, planes, owners_in), grid=(i...  11 us

profile of v2, /device:TPU:1, one launch (start us, length us, event | category | flops | bytes accessed | tf_op | source)
XLA Modules:
  0.0 139.4 jit_solution(2209291282363812479)
XLA Ops:
  0.0 0.0 copy-start.1
  0.0 11.0 %shard_map.30 = (bf16[8,176,1024]{2,1,0:T(8,128)(2,1)S(1)}, f32[8,8,256]{2,1,0:T(8,128)S(1)}, s32[8,1024]{1,0:T(8,128)S(1)}) custom-call(s32[1,1024]{1,0:T(1,128)} %bitcast.26, bf16[1024,4096]{1,0:T(8,128)(2,1)} %x_ref.1), custom_call_target="tpu_custom_call" | custom-call | tf_op jit(solution)/shard_map/pallas_call | solution.py:101
  11.0 0.0 copy-start
  11.0 1.6 %copy-done = bf16[8,176,1024]{2,1,0:T(8,128)(2,1)} copy-done((bf16[8,176,1024]{2,1,0:T(8,128)(2,1)}, bf16[8,176,1024]{2,1,0:T(8,128)(2,1)S(1)}, u32[]{:S(2)}) %copy-start) | copy-done | bytes 2883608
  12.6 124.6 %shard_map.31 = f32[1,1024]{1,0:T(1,128)S(1)} custom-call(bf16[8,176,1024]{2,1,0:T(8,128)(2,1)} %copy-done, f32[8,8,256]{2,1,0:T(8,128)S(1)} %get-tuple-element.21.lids_ref, s32[8,1024]{1,0:T(8,128)S(1)} %get-tuple-element.22.index_ref), custom_call_target="tpu_custom_call" | custom-call | tf_op jit(solution)/shard_map/pallas_call | solution.py:482
  137.2 0.6 reduce_max.18
  138.5 0.0 copy-done.1
  138.5 0.3 conditional.1
  138.8 0.6 copy.16
Async XLA Ops:
  0.0 138.5 %copy-start.1 = (s32[1024]{0:T(1024)S(1)}, s32[1024]{0:T(1024)}, u32[]{:S(2)}) copy-start(s32[1024]{0:T(1024)} %param.5) | copy-start | bytes 12292
  11.0 1.6 %copy-start = (bf16[8,176,1024]{2,1,0:T(8,128)(2,1)}, bf16[8,176,1024]{2,1,0:T(8,128)(2,1)S(1)}, u32[]{:S(2)}) copy-start(bf16[8,176,1024]{2,1,0:T(8,128)(2,1)S(1)} %get-tuple-element.20.packed_ref) | copy-start | bytes 8650756

commit v3 on v0

--- a/solution.py
+++ b/solution.py
@@ -1,9 +1,583 @@
+import functools
+
 import jax
 import jax.numpy as jnp
 from jax import lax
+from jax.experimental import pallas as pl
+from jax.experimental.pallas import tpu as pltpu
 from jax.sharding import PartitionSpec as P
 
 CLU_OWN = 8
+SLOTS = 32
+Z_SLOTS = 176
+BLOCK = 128
+LATE = 3
+FEW = 64
+MANY = 2 * BLOCK
+CAP = MANY + LATE * FEW
+STARTS = (0, MANY, MANY + FEW, MANY + 2 * FEW)
+SCORE_ROWS = (4 * BLOCK, 2 * BLOCK + FEW, 3 * BLOCK, 3 * BLOCK + FEW)
+TOO_MANY = 4.0 * CLU_OWN
+F32 = jnp.float32
+BF16 = jnp.bfloat16
+MESH = pl.DeviceIdType.MESH
+NN = (((1,), (0,)), ((), ()))
+NT = (((1,), (1,)), ((), ()))
+
+
+def dot(a, b, dims=NN, precision=None):
+    return lax.dot_general(a, b, dims, preferred_element_type=F32, precision=precision)
+
+
+def iota(shape, dim):
+    return lax.broadcasted_iota(jnp.int32, shape, dim)
+
+
+def hot(cond):
+    return jnp.where(cond, 1.0, 0.0).astype(BF16)
+
+
+def nearest_first(n):
+    order = [0]
+    for d in range(1, n // 2 + 1):
+        order += [d] if 2 * d == n else [d, n - d]
+    return order
+
+
+def highest(score, limit):
+    return jnp.max(jnp.where(limit, score, -1.0), axis=0, keepdims=True)
+
+
+def most(a):
+    return jnp.max(jnp.max(a, axis=1, keepdims=True), axis=0, keepdims=True)
+
+
+def kernel(
+    planes,
+    owners_in,
+    ids_ref,
+    x_ref,
+    out_ref,
+    flag_ref,
+    x_rows,
+    unit,
+    index,
+    packed,
+    z_rows,
+    lids_own,
+    z_lids,
+    lids_out,
+    x_lids,
+    staged,
+    rows,
+    sorted_rows,
+    partial,
+    relay,
+    near,
+    far,
+    forward,
+    values_out,
+    x_back,
+    values_home,
+    z_back,
+    load_sem,
+    z_send,
+    z_recv,
+    zl_send,
+    zl_recv,
+    xl_send,
+    xl_recv,
+    x_send,
+    x_recv,
+    y_send,
+    y_recv,
+    xb_send,
+    xb_recv,
+    zb_send,
+    zb_recv,
+):
+    lanes = owners_in * SLOTS
+    owners = planes * owners_in
+    items = ids_ref.shape[1]
+    blocks, _, width = x_rows.shape
+    part = unit.shape[1]
+    me = lax.axis_index("prod")
+    tile = lax.axis_index("tile")
+    my_plane = me // owners_in
+    my_col = lax.rem(me, owners_in)
+    at_plane = lambda d: lax.rem(my_plane + d, planes)
+    at_col = lambda k: lax.rem(my_col + k, owners_in)
+    at_tile = lambda k: lax.rem(tile + k, 4)
+    to_plane = lambda d: {"prod": at_plane(d) * owners_in + my_col}
+    to_col = lambda k: {"prod": my_plane * owners_in + at_col(k)}
+    to_tile = lambda k: {"tile": at_tile(k)}
+    to_both = lambda k, j: {"prod": my_plane * owners_in + at_col(k), "tile": at_tile(j)}
+    order = nearest_first(planes)
+    first_late = planes - LATE
+    started = []
+
+    def send(src, dst, send_sem, recv_sem, device):
+        copy = pltpu.make_async_remote_copy(
+            src_ref=src,
+            dst_ref=dst,
+            send_sem=send_sem,
+            recv_sem=recv_sem,
+            device_id=device,
+            device_id_type=MESH,
+        )
+        copy.start()
+        started.append(copy)
+        return copy
+
+    loads = [
+        pltpu.make_async_copy(
+            x_ref.at[pl.ds(n * BLOCK, BLOCK)], x_rows.at[n], load_sem.at[n]
+        )
+        for n in range(blocks)
+    ]
+    for load in loads:
+        load.start()
+
+    barrier = pltpu.get_barrier_semaphore()
+    for d in range(1, planes):
+        pl.semaphore_signal(barrier, inc=1, device_id=to_plane(d), device_id_type=MESH)
+    for k in range(owners_in):
+        for j in range(4):
+            if k or j:
+                pl.semaphore_signal(
+                    barrier, inc=1, device_id=to_both(k, j), device_id_type=MESH
+                )
+
+    ids = ids_ref[...]
+    owner = ids // CLU_OWN
+    plane = owner // owners_in
+    lid = lax.rem(ids, CLU_OWN)
+    owned = jnp.where(iota((owners, items), 0) == owner, 1.0, 0.0)
+    before_block = hot(iota((BLOCK, BLOCK), 0) < iota((BLOCK, BLOCK), 1))
+    count = jnp.zeros((owners, 1), F32)
+    ahead = []
+    for n in range(items // BLOCK):
+        block = owned[:, n * BLOCK : (n + 1) * BLOCK]
+        ahead.append(dot(block.astype(BF16), before_block) + count)
+        count += jnp.sum(block, axis=1, keepdims=True)
+    ahead = jnp.concatenate(ahead, axis=1)
+    a, b = (iota((owners, owners), n) for n in (0, 1))
+    lower = hot((a // owners_in == b // owners_in) & (b < a))
+    offset = dot(lower, jnp.broadcast_to(count, (owners, BLOCK)).astype(BF16))[:, :1]
+    slot = jnp.sum(owned * ahead, axis=0, keepdims=True).astype(jnp.int32)
+    position = jnp.sum(owned * (ahead + offset), axis=0, keepdims=True).astype(jnp.int32)
+    place = lax.rem(owner, owners_in) * SLOTS + slot
+    row = iota((8, items), 0)
+    index[...] = jnp.where(
+        row == 0, lax.rem(plane - my_plane + planes, planes), jnp.where(row == 1, place, position)
+    )
+    by_plane = jnp.where(iota((planes, items), 0) == plane, lid + 1, 0).astype(F32).astype(BF16)
+    by_place = hot(iota((lanes, items), 0) == place)
+    lids = dot(by_plane, by_place, NT)
+    lids += jnp.where(jnp.max(position, axis=1, keepdims=True) >= Z_SLOTS, TOO_MANY, 0.0)
+    for z in range(planes):
+        lids_own[z] = jnp.broadcast_to(lids[z : z + 1], lids_own.shape[1:])
+
+    def unit_rows(n, carry):
+        pltpu.make_async_copy(
+            x_ref.at[pl.ds(pl.multiple_of(n * BLOCK, BLOCK), BLOCK)], x_rows.at[n], load_sem.at[n]
+        ).wait()
+        total = jnp.zeros((BLOCK, BLOCK), F32)
+        for c in range(width // BLOCK):
+            x = x_rows[n, :, c * BLOCK : (c + 1) * BLOCK].astype(F32)
+            total += x * x
+        scale = lax.rsqrt(jnp.sum(total, axis=1, keepdims=True) + 1e-06)
+        mine = x_rows[n, :, pl.ds(pl.multiple_of(tile * part, part), part)].astype(F32)
+        unit[pl.ds(pl.multiple_of(n * BLOCK, BLOCK), BLOCK), :] = (mine * scale).astype(BF16)
+        return carry
+
+    lax.fori_loop(0, blocks, unit_rows, 0)
+
+    pl.semaphore_wait(barrier, planes - 1 + 4 * owners_in - 1)
+    lid_copies = [
+        send(lids_own.at[at_plane(d)], z_lids.at[d], zl_send.at[d], zl_recv.at[d], to_plane(d))
+        for d in order[1:]
+    ]
+    row_copies = {}
+    for d in order[1:3] + order[:1] + order[3:]:
+        wanted = jnp.where(index[0:1, :] == d, index[2:3, :], -1)
+        chosen = dot(hot(iota((Z_SLOTS, items), 0) == wanted), unit[...]).astype(BF16)
+        if d == 0:
+            z_rows[0] = chosen
+        else:
+            packed[d] = chosen
+            row_copies[d] = send(
+                packed.at[d], z_rows.at[d], z_send.at[d], z_recv.at[d], to_plane(d)
+            )
+
+    for copy in lid_copies:
+        copy.wait_recv()
+    lids = jnp.concatenate(
+        [lids_own[my_plane][0:1]] + [z_lids[d][0:1] for d in range(1, planes)], axis=0
+    )
+    lids_out[...] = pltpu.roll(lids, lax.rem(owners_in - my_col, owners_in) * SLOTS, 1)
+    col_lid_copies = [
+        send(lids_out, x_lids.at[k], xl_send.at[k], xl_recv.at[k], to_col(k))
+        for k in range(1, owners_in)
+    ]
+    before = hot(iota((lanes, lanes), 0) < iota((lanes, lanes), 1))
+    rank = dot(hot(lids > 0.0), before)
+    source = jnp.where(lids > 0.0, rank, -1.0)
+    source = jnp.concatenate([source, jnp.zeros((BLOCK - planes, lanes), F32)], axis=0).T
+
+    def forward_rows(d):
+        if d:
+            row_copies[d].wait_recv()
+        take = source[:, d : d + 1].astype(jnp.int32) == iota((lanes, Z_SLOTS), 1)
+        staged[d] = dot(hot(take), z_rows[d]).astype(BF16)
+        copies = []
+        for k in range(owners_in):
+            start = pl.multiple_of(at_col(k) * SLOTS, SLOTS)
+            src = staged.at[d, pl.ds(start, SLOTS)]
+            dst = rows.at[d, pl.ds(k * SLOTS, SLOTS)]
+            if k == 0:
+                copy = pltpu.make_async_copy(src, dst, x_recv.at[d, 0])
+                copy.start()
+            else:
+                copy = send(src, dst, x_send.at[d, k], x_recv.at[d, k], to_col(k))
+            copies.append(copy)
+        return copies
+
+    x_copies = {order[0]: forward_rows(order[0])}
+
+    for copy in col_lid_copies:
+        copy.wait_recv()
+    got = jnp.zeros((planes, lanes), F32)
+    marks = lids_out[...]
+    group = iota((planes, lanes), 1) // SLOTS
+    for k in range(owners_in):
+        theirs = lids_out[...] if k == 0 else x_lids[k]
+        got += jnp.where(group == k, theirs, 0.0)
+        marks = jnp.maximum(marks, theirs)
+
+    def set_of(d):
+        which = jnp.zeros(d.shape, jnp.int32)
+        for n in range(LATE):
+            which = jnp.where(d == order[first_late + n], n + 1, which)
+        return which
+
+    member = jnp.concatenate([hot(got == c + 1.0) for c in range(CLU_OWN)], axis=0)
+    in_row = dot(member, before)
+    in_rows = dot(member, jnp.ones((lanes, lanes), BF16)).astype(BF16)
+    a, b = (iota((CLU_OWN * planes, CLU_OWN * planes), n) for n in (0, 1))
+    same = (a // planes == b // planes) & (set_of(lax.rem(a, planes)) == set_of(lax.rem(b, planes)))
+    rank_all = in_row + dot(hot(same & (b < a)), in_rows)
+    a, b = (iota((CLU_OWN * (LATE + 1), CLU_OWN * planes), n) for n in (0, 1))
+    same = (lax.rem(a, CLU_OWN) == b // planes) & (a // CLU_OWN == set_of(lax.rem(b, planes)))
+    sizes = dot(hot(same), in_rows)
+    unfit = (
+        (most(marks) >= TOO_MANY)
+        | (most(sizes[:CLU_OWN]) > MANY)
+        | (most(sizes[CLU_OWN:]) > FEW)
+    )
+    ranked = jnp.zeros((planes, lanes), F32)
+    for c in range(CLU_OWN):
+        this = slice(c * planes, (c + 1) * planes)
+        ranked += jnp.where(got == c + 1.0, rank_all[this], 0.0)
+    late = set_of(iota((planes, lanes), 0))
+    cluster = got.astype(jnp.int32) - 1
+    ranked = ranked.astype(jnp.int32)
+    target = jnp.where(cluster >= 0, cluster * jnp.where(late == 0, MANY, FEW) + ranked, -1)
+
+    def place_rows(n):
+        d = order[n]
+        copies = x_copies[d]
+        copies[0].wait()
+        for copy in copies[1:]:
+            copy.wait_recv()
+        goal = target[d : d + 1]
+        if n >= first_late:
+            moved = dot(hot(iota((CLU_OWN * FEW, lanes), 0) == goal), rows[d]).astype(BF16)
+            start = STARTS[n - first_late + 1]
+            for c in range(CLU_OWN):
+                sorted_rows[c, start : start + FEW, :] = moved[c * FEW : (c + 1) * FEW]
+            return
+
+        def body(c, carry):
+            chosen = hot(iota((MANY, lanes), 0) + c * MANY == goal)
+            moved = dot(chosen, rows[d]).astype(BF16)
+            if n:
+                sorted_rows[c, :MANY, :] = sorted_rows[c, :MANY, :] + moved
+            else:
+                sorted_rows[c, :MANY, :] = moved
+            return carry
+
+        lax.fori_loop(0, CLU_OWN, body, 0)
+
+    r, c = (iota((BLOCK, BLOCK), n) for n in (0, 1))
+    right, left, across = at_tile(1), at_tile(3), at_tile(2)
+    spans = []
+    for s, n in enumerate(SCORE_ROWS):
+        spans.append((sum(SCORE_ROWS[:s]), n // 2))
+
+    def scores(t, s):
+        base = spans[s][0]
+        if s == 0:
+            for j in range(2):
+                block = sorted_rows[2 * t + j, :MANY, :]
+                all_pairs = dot(block, block, NT)
+                at = base + 2 * j * BLOCK
+                partial[t, at : at + BLOCK] = all_pairs[:BLOCK, BLOCK:]
+                partial[t, at + BLOCK : at + 2 * BLOCK] = jnp.where(
+                    c > r, all_pairs[:BLOCK, :BLOCK], all_pairs[BLOCK:, BLOCK:]
+                )
+            return
+        start, stop = STARTS[s], STARTS[s] + FEW
+        full = stop // BLOCK
+        ends = []
+        for j in range(2):
+            new = sorted_rows[2 * t + j, start:stop, :]
+            pairs = dot(new, sorted_rows[2 * t + j, : full * BLOCK, :], NT)
+            for p in range(full):
+                at = base + p * BLOCK + j * FEW
+                partial[t, at : at + FEW] = pairs[:, p * BLOCK : (p + 1) * BLOCK]
+            if stop % BLOCK:
+                ends.append(dot(new, sorted_rows[2 * t + j, start - FEW : stop, :], NT))
+        if ends:
+            at = base + full * BLOCK
+            partial[t, at : at + FEW] = jnp.where(
+                c[:FEW] < FEW, pltpu.roll(ends[0], FEW, 1), ends[1]
+            )
+
+    y_copies = {}
+
+    def y_send_to(s, n, src, dst, step):
+        y_copies[s, n] = send(src, dst, y_send.at[s, n], y_recv.at[s, n], to_tile(step))
+
+    def begin_sum(s):
+        base, half = spans[s]
+        head, tail, at = pl.ds(base, half), pl.ds(base + half, half), pl.ds(base // 2, half)
+        scores(across, s)
+        y_send_to(s, 0, partial.at[across, head], relay.at[0, at], 1)
+        y_send_to(s, 1, partial.at[across, tail], relay.at[1, at], 3)
+        scores(right, s)
+        y_send_to(s, 2, partial.at[right, tail], near.at[1, at], 1)
+        scores(left, s)
+        y_send_to(s, 3, partial.at[left, head], near.at[0, at], 3)
+        scores(tile, s)
+
+    def relay_sum(s):
+        base, half = spans[s]
+        at = pl.ds(base // 2, half)
+        y_copies[s, 0].wait_recv()
+        forward[0, at] = relay[0, at] + partial[right, pl.ds(base, half)]
+        y_send_to(s, 4, forward.at[0, at], far.at[0, at], 1)
+        y_copies[s, 1].wait_recv()
+        forward[1, at] = relay[1, at] + partial[left, pl.ds(base + half, half)]
+        y_send_to(s, 5, forward.at[1, at], far.at[1, at], 3)
+
+    def end_sum(s):
+        base, half = spans[s]
+        at = pl.ds(base // 2, half)
+        for n in range(2, 6):
+            y_copies[s, n].wait_recv()
+        return jnp.concatenate(
+            [partial[tile, pl.ds(base + h * half, half)] + near[h, at] + far[h, at] for h in (0, 1)],
+            axis=0,
+        )
+
+    size_row = iota((BLOCK, lanes), 0)[: CLU_OWN * (LATE + 1)]
+    size = [
+        [
+            jnp.sum(
+                jnp.where(size_row == s * CLU_OWN + 2 * tile + j, sizes, 0.0), axis=0, keepdims=True
+            )[:, :BLOCK].astype(jnp.int32)
+            for j in range(2)
+        ]
+        for s in range(LATE + 1)
+    ]
+    lane = iota((1, BLOCK), 1)
+    size_both = [jnp.where(lane < FEW, a, b) for a, b in size]
+    by_column = {}
+    by_new = {}
+
+    def raise_to(j, p, value):
+        by_column[j, p] = jnp.maximum(by_column[j, p], value) if (j, p) in by_column else value
+
+    def best_of(s):
+        total = end_sum(s)
+        if s == 0:
+            above, below = c > r, c < r
+            for j in range(2):
+                cross = total[2 * j * BLOCK : (2 * j + 1) * BLOCK]
+                fold = total[(2 * j + 1) * BLOCK : (2 * j + 2) * BLOCK]
+                turned = fold.T
+                low, high = r < size[0][j], r + BLOCK < size[0][j]
+                raise_to(j, 0, highest(fold, low & above))
+                raise_to(j, 0, highest(turned, low & below))
+                raise_to(j, 0, highest(cross.T, high))
+                raise_to(j, 1, highest(fold, high & below))
+                raise_to(j, 1, highest(turned, high & above))
+                raise_to(j, 1, highest(cross, low))
+            return
+        start, stop = STARTS[s], STARTS[s] + FEW
+        full = stop // BLOCK
+        row_few, col_few = r[:FEW], c[:FEW]
+        news = []
+        for p in range(full):
+            tile_p = total[p * BLOCK : (p + 1) * BLOCK]
+            for j in range(2):
+                limit = row_few < size[s][j]
+                if (p + 1) * BLOCK == stop:
+                    limit = limit & (col_few - FEW != row_few)
+                raise_to(j, p, highest(tile_p[j * FEW : (j + 1) * FEW], limit))
+            if p < 2:
+                earlier = r + p * BLOCK < size_both[0]
+            else:
+                earlier = (r < FEW) & (r < size_both[1])
+                if s == 3:
+                    earlier = earlier | ((r >= FEW) & (r - FEW < size_both[2]))
+            news.append(highest(tile_p.T, earlier))
+        if stop % BLOCK:
+            limit = (row_few < size_both[s]) & (row_few != lax.rem(col_few, FEW))
+            news.append(highest(total[full * BLOCK :], limit))
+        by_new[s] = functools.reduce(jnp.maximum, news)
+
+    for n in range(planes):
+        if n:
+            x_copies[order[n]] = forward_rows(order[n])
+            place_rows(n - 1)
+            s = n - first_late
+            if s == 0:
+                begin_sum(0)
+            elif s > 0:
+                relay_sum(s - 1)
+                begin_sum(s)
+                if s >= 2:
+                    best_of(s - 2)
+    place_rows(planes - 1)
+    relay_sum(LATE - 1)
+    begin_sum(LATE)
+    best_of(LATE - 2)
+    relay_sum(LATE)
+    best_of(LATE - 1)
+    best_of(LATE)
+
+    swap = lambda v: pltpu.roll(v, FEW, 1)
+    low = lane < FEW
+    raise_to(0, 2, jnp.where(low, by_new[1], swap(by_new[2])))
+    raise_to(1, 2, jnp.where(low, swap(by_new[1]), by_new[2]))
+    raise_to(0, 3, by_new[3])
+    raise_to(1, 3, swap(by_new[3]))
+    table = jnp.concatenate([by_column[j, p] for j in range(2) for p in range(4)], axis=0)
+    table = jnp.concatenate([table, jnp.zeros((BLOCK - 8, BLOCK), F32)], axis=0).T
+
+    where = ranked
+    for s in range(1, LATE + 1):
+        where = where + jnp.where(late == s, STARTS[s], 0)
+    where_row = lax.rem(cluster + 2, 2) * 4 + where // BLOCK
+    where_row = jnp.where((cluster >= 0) & (cluster // 2 == tile), where_row, -1)
+    where_lane = lax.rem(where, BLOCK)
+    picked = []
+    for d in range(planes):
+        values = jnp.zeros((BLOCK, lanes), F32)
+        for n in range(8):
+            values = jnp.where(where_row[d : d + 1] == n, table[:, n : n + 1], values)
+        mask = iota((BLOCK, lanes), 0) == where_lane[d : d + 1]
+        picked.append(jnp.sum(jnp.where(mask, values, 0.0), axis=0, keepdims=True))
+    values_out[...] = jnp.where(unfit, TOO_MANY, jnp.concatenate(picked, axis=0))
+    col_back = [
+        send(
+            values_out,
+            x_back.at[j, k],
+            xb_send.at[j, k],
+            xb_recv.at[j, k],
+            to_both(owners_in - k, j),
+        )
+        for k in range(owners_in)
+        for j in range(4)
+        if k or j
+    ]
+    home = jnp.where(group == 0, values_out[...], 0.0)
+    for copy in col_back:
+        copy.wait_recv()
+    for k in range(owners_in):
+        for j in range(4):
+            if k or j:
+                home += jnp.where(group == k, x_back[j, k], 0.0)
+    values_home[...] = pltpu.roll(home, my_col * SLOTS, 1)
+    plane_back = [
+        send(values_home, z_back.at[d], zb_send.at[d], zb_recv.at[d], to_plane(planes - d))
+        for d in range(1, planes)
+    ]
+    for copy in plane_back:
+        copy.wait_recv()
+    marks = values_home[...]
+    for d in range(1, planes):
+        marks = jnp.maximum(marks, z_back[d])
+    flag_ref[0, 0] = jnp.max(marks)
+    mine = jnp.concatenate(
+        [values_home[0:1]] + [z_back[d][d : d + 1] for d in range(1, planes)], axis=0
+    )
+    mine = jnp.concatenate([mine, jnp.zeros((BLOCK - planes, lanes), F32)], axis=0).T
+    chosen = jnp.where(iota((BLOCK, items), 0) == index[0:1, :], 1.0, 0.0)
+    values = dot(mine, chosen, precision=lax.Precision.HIGHEST)
+    mask = iota((lanes, items), 0) == index[1:2, :]
+    out_ref[...] = jnp.sum(jnp.where(mask, values, 0.0), axis=0, keepdims=True)
+
+    for copy in started:
+        copy.wait_send()
+
+
+def fast(planes, owners_in, embeddings, cluster_ids, part):
+    items, width = embeddings.shape
+    lanes = owners_in * SLOTS
+    total = sum(SCORE_ROWS)
+    vmem = pl.BlockSpec(memory_space=pltpu.VMEM)
+    dma = lambda *shape: pltpu.SemaphoreType.DMA(shape)
+    buffer = pltpu.VMEM
+    return pl.pallas_call(
+        functools.partial(kernel, planes, owners_in),
+        out_shape=(jax.ShapeDtypeStruct((1, items), F32), jax.ShapeDtypeStruct((1, 1), F32)),
+        in_specs=[vmem, pl.BlockSpec(memory_space=pl.ANY)],
+        out_specs=(vmem, pl.BlockSpec(memory_space=pltpu.SMEM)),
+        scratch_shapes=[
+            buffer((items // BLOCK, BLOCK, width), BF16),
+            buffer((items, part), BF16),
+            buffer((8, items), jnp.int32),
+            buffer((planes, Z_SLOTS, part), BF16),
+            buffer((planes, Z_SLOTS, part), BF16),
+            buffer((planes, 8, lanes), F32),
+            buffer((planes, 8, lanes), F32),
+            buffer((planes, lanes), F32),
+            buffer((owners_in, planes, lanes), F32),
+            buffer((planes, lanes, part), BF16),
+            buffer((planes, lanes, part), BF16),
+            buffer((CLU_OWN, CAP, part), BF16),
+            buffer((4, total, BLOCK), F32),
+            buffer((2, total // 2, BLOCK), F32),
+            buffer((2, total // 2, BLOCK), F32),
+            buffer((2, total // 2, BLOCK), F32),
+            buffer((2, total // 2, BLOCK), F32),
+            buffer((planes, lanes), F32),
+            buffer((4, owners_in, planes, lanes), F32),
+            buffer((planes, lanes), F32),
+            buffer((planes, planes, lanes), F32),
+            dma(items // BLOCK),
+            dma(planes),
+            dma(planes),
+            dma(planes),
+            dma(planes),
+            dma(owners_in),
+            dma(owners_in),
+            dma(planes, owners_in),
+            dma(planes, owners_in),
+            dma(LATE + 1, 6),
+            dma(LATE + 1, 6),
+            dma(4, owners_in),
+            dma(4, owners_in),
+            dma(planes),
+            dma(planes),
+        ],
+        compiler_params=pltpu.CompilerParams(
+            collective_id=0, has_side_effects=True, vmem_limit_bytes=60 * 1024 * 1024
+        ),
+    )(cluster_ids.reshape(1, items), embeddings)
 
 
 def pair_best(row_block, row_labels, columns, column_labels, column_start):
@@ -20,13 +594,12 @@
     return jnp.max(jnp.where(in_cluster, scores, -1.0), axis=1)
 
 
-def shards(embeddings, cluster_ids):
+def any_layout(embeddings, cluster_ids):
     prod_count = lax.axis_size("prod")
     tile_count = lax.axis_size("tile")
     item_dev = embeddings.shape[0]
     width = embeddings.shape[1]
-    per_owner = 2 * item_dev // prod_count
-    group_rows = prod_count * per_owner
+    group_rows = prod_count * SLOTS
     widened = embeddings.astype(jnp.float32)
     normed = (
         widened * lax.rsqrt(jnp.sum(widened * widened, axis=1, keepdims=True) + 1e-06)
@@ -37,7 +610,7 @@
     )
     running = jnp.cumsum(owner_hot, axis=0)
     slot_index = jnp.sum(running * owner_hot, axis=1) - 1
-    position = owners * per_owner + slot_index
+    position = owners * SLOTS + slot_index
     inverse = (
         jnp.full((group_rows,), item_dev, jnp.int32)
         .at[position]
@@ -45,8 +618,8 @@
     )
     padded = jnp.concatenate([normed, jnp.zeros((1, width), jnp.bfloat16)], axis=0)
     labels = jnp.concatenate([cluster_ids, jnp.full((1,), -1, jnp.int32)], axis=0)
-    outgoing = padded[inverse].reshape(prod_count, per_owner, width)
-    out_labels = labels[inverse].reshape(prod_count, per_owner)
+    outgoing = padded[inverse].reshape(prod_count, SLOTS, width)
+    out_labels = labels[inverse].reshape(prod_count, SLOTS)
     tile_pos = lax.axis_index("tile")
     row_block, row_labels = (
         lax.all_to_all(outgoing, "prod", split_axis=0, concat_axis=0, tiled=True),
@@ -66,6 +639,23 @@
     return returned.reshape(group_rows)[position]
 
 
+def shards(embeddings, cluster_ids):
+    prod_count = lax.axis_size("prod")
+    owners_in = 8 if prod_count >= 64 else 4
+    planes = prod_count // owners_in
+    part = embeddings.shape[1] // lax.axis_size("tile")
+    best, mark = fast(planes, owners_in, embeddings, cluster_ids, part)
+    fits = mark[0, 0] < TOO_MANY
+    return lax.cond(
+        fits,
+        lambda e, i, b: b,
+        lambda e, i, b: any_layout(e, i),
+        embeddings,
+        cluster_ids,
+        best.reshape(-1),
+    )
+
+
 def solution(mesh):
     placed = (P("prod", None), P("prod"))
     return jax.shard_map(shards, mesh=mesh, in_specs=placed, out_specs=P("prod"), check_vma=False)

time: 549 us -> 126 us (0.23)
  waiting for transfers between devices: 363 us -> 0 us
  Pallas kernels: 0 us -> 125 us
  local copies, waits for them, and re-layouts: 69.9 us -> 0.6 us
  blocking collectives: 39.3 us -> 0 us
  other arithmetic: 36.8 us -> 0 us
  starting transfers between devices: 23.5 us -> 0 us
  matrix products: 16.4 us -> 0 us
    all_to_all x2 -> x0, waiting for transfers between devices: 363 us -> none  [the longest x1 363 us: shards(): lax.all_to_all(outgoing, 'prod', split_axis=0, concat_axis=0, tiled=True)]
    pallas_call x0 -> x1, Pallas kernels: none -> 125 us  [fast(): pl.pallas_call(functools.partial(kernel, planes, owners_in), out_shape=(j...]
    gather x3 -> x0, local copies, waits for them, and re-layouts: 55.5 us -> none  [the longest x1 33.1 us: shards(): outgoing = padded[inverse].reshape(prod_count, per_owner, width)]
    all_to_all x1 -> x0, blocking collectives: 28 us -> none  [shards(): lax.all_to_all(maxima.reshape(prod_count, -1), 'prod', split_axis=0, conc...]
    all_to_all x2 -> x0, starting transfers between devices: 23.5 us -> none  [the longest x1 13 us: shards(): lax.all_to_all(out_labels, 'prod', split_axis=0, concat_axis=0, tiled=True)]
    another operation x3 -> x0, other arithmetic: 18.2 us -> none
    dot_general x1 -> x0, matrix products: 16.4 us -> none  [pair_best(): lax.dot_general(row_block, columns, (((1,), (1,)), ((), ())), preferred_e...]
    pmax x1 -> x0, blocking collectives: 11.4 us -> none  [shards(): maxima = lax.pmax(partial_best, 'tile')]
  transfers between devices with their start and end apart: 2 -> 0, of which waited for: 1 -> 0; matrix products, arithmetic and copies ran while one was open for 10% -> 0% of each run, Pallas kernels for 0% -> 0%
where the time goes in v3:
time: 126 us
  Pallas kernels  125 us (99%)
    pallas_call x1, Pallas kernels, fast(): pl.pallas_call(functools.partial(kernel, planes, owners_in), out_shape=(j...  125 us

profile of v3, /device:TPU:1, one launch (start us, length us, event | category | flops | bytes accessed | tf_op | source)
XLA Modules:
  0.0 126.3 jit_solution(7962324794011066677)
XLA Ops:
  0.0 124.8 %shard_map.30 = (f32[1,1024]{1,0:T(1,128)S(1)}, f32[1,1]{1,0:T(1,128)}) custom-call(s32[1,1024]{1,0:T(1,128)} %bitcast.27, bf16[1024,4096]{1,0:T(8,128)(2,1)} %x_ref.1), custom_call_target="tpu_custom_call" | custom-call | tf_op jit(solution)/shard_map/pallas_call | solution.py:534
  125.4 0.3 conditional.1
  125.7 0.6 copy.16

commit v4 on v3

--- a/solution.py
+++ b/solution.py
@@ -10,6 +10,8 @@
 CLU_OWN = 8
 SLOTS = 32
 Z_SLOTS = 176
+NEAR_SLOTS = SLOTS // 2
+FAR_SLOTS = 48
 BLOCK = 128
 LATE = 3
 FEW = 64
@@ -70,6 +72,8 @@
     x_lids,
     staged,
     rows,
+    far_rows,
+    last_rows,
     sorted_rows,
     partial,
     relay,
@@ -89,6 +93,8 @@
     xl_recv,
     x_send,
     x_recv,
+    far_send,
+    far_recv,
     y_send,
     y_recv,
     xb_send,
@@ -111,9 +117,11 @@
     to_plane = lambda d: {"prod": at_plane(d) * owners_in + my_col}
     to_col = lambda k: {"prod": my_plane * owners_in + at_col(k)}
     to_tile = lambda k: {"tile": at_tile(k)}
+    to_far = lambda k: {"prod": at_plane(far_plane) * owners_in + at_col(k)}
     to_both = lambda k, j: {"prod": my_plane * owners_in + at_col(k), "tile": at_tile(j)}
     order = nearest_first(planes)
-    first_late = planes - LATE
+    far_plane = order[-1]
+    first_late = planes - LATE + 1
     started = []
 
     def send(src, dst, send_sem, recv_sem, device):
@@ -138,9 +146,16 @@
     for load in loads:
         load.start()
 
+    for k in range(owners_in):
+        blank = jnp.zeros((NEAR_SLOTS, part), BF16)
+        rows[far_plane, k * SLOTS : k * SLOTS + NEAR_SLOTS, :] = blank
+        last_rows[k * SLOTS + NEAR_SLOTS : (k + 1) * SLOTS, :] = blank
+
     barrier = pltpu.get_barrier_semaphore()
     for d in range(1, planes):
         pl.semaphore_signal(barrier, inc=1, device_id=to_plane(d), device_id_type=MESH)
+    for k in range(1, owners_in):
+        pl.semaphore_signal(barrier, inc=1, device_id=to_far(k), device_id_type=MESH)
     for k in range(owners_in):
         for j in range(4):
             if k or j:
@@ -166,15 +181,21 @@
     offset = dot(lower, jnp.broadcast_to(count, (owners, BLOCK)).astype(BF16))[:, :1]
     slot = jnp.sum(owned * ahead, axis=0, keepdims=True).astype(jnp.int32)
     position = jnp.sum(owned * (ahead + offset), axis=0, keepdims=True).astype(jnp.int32)
-    place = lax.rem(owner, owners_in) * SLOTS + slot
-    row = iota((8, items), 0)
-    index[...] = jnp.where(
-        row == 0, lax.rem(plane - my_plane + planes, planes), jnp.where(row == 1, place, position)
-    )
+    spill = jnp.broadcast_to(jnp.maximum(count - NEAR_SLOTS, 0.0), (owners, BLOCK)).astype(BF16)
+    spill = jnp.sum(owned * dot(lower, spill)[:, :1], axis=0, keepdims=True).astype(jnp.int32)
+    column = lax.rem(owner, owners_in)
+    place = column * SLOTS + slot
+    away = lax.rem(plane - my_plane + planes, planes)
+    direct = jnp.where(slot < NEAR_SLOTS, column * NEAR_SLOTS + slot, -1)
+    spilled = jnp.where(slot < NEAR_SLOTS, -1, spill + slot - NEAR_SLOTS)
+    for n, line in enumerate((away, place, position, direct, spilled)):
+        index[n : n + 1, :] = line
+    room = (position < Z_SLOTS) & ((away != far_plane) | (spilled < FAR_SLOTS))
+    crowded = jnp.max(jnp.where(room, 0.0, TOO_MANY), axis=1, keepdims=True)
     by_plane = jnp.where(iota((planes, items), 0) == plane, lid + 1, 0).astype(F32).astype(BF16)
     by_place = hot(iota((lanes, items), 0) == place)
     lids = dot(by_plane, by_place, NT)
-    lids += jnp.where(jnp.max(position, axis=1, keepdims=True) >= Z_SLOTS, TOO_MANY, 0.0)
+    lids += crowded
     for z in range(planes):
         lids_own[z] = jnp.broadcast_to(lids[z : z + 1], lids_own.shape[1:])
 
@@ -193,22 +214,43 @@
 
     lax.fori_loop(0, blocks, unit_rows, 0)
 
-    pl.semaphore_wait(barrier, planes - 1 + 4 * owners_in - 1)
+    pl.semaphore_wait(barrier, planes - 1 + owners_in - 1 + 4 * owners_in - 1)
     lid_copies = [
         send(lids_own.at[at_plane(d)], z_lids.at[d], zl_send.at[d], zl_recv.at[d], to_plane(d))
         for d in order[1:]
     ]
     row_copies = {}
-    for d in order[1:3] + order[:1] + order[3:]:
-        wanted = jnp.where(index[0:1, :] == d, index[2:3, :], -1)
-        chosen = dot(hot(iota((Z_SLOTS, items), 0) == wanted), unit[...]).astype(BF16)
-        if d == 0:
-            z_rows[0] = chosen
-        else:
-            packed[d] = chosen
-            row_copies[d] = send(
-                packed.at[d], z_rows.at[d], z_send.at[d], z_recv.at[d], to_plane(d)
+
+    def chosen_rows(d, line, count):
+        wanted = jnp.where(index[0:1, :] == d, index[line : line + 1, :], -1)
+        return dot(hot(iota((count, items), 0) == wanted), unit[...]).astype(BF16)
+
+    def send_rows(d, line, count):
+        packed[d, :count, :] = chosen_rows(d, line, count)
+        at = pl.ds(0, count)
+        row_copies[d] = send(
+            packed.at[d, at], z_rows.at[d, at], z_send.at[d], z_recv.at[d], to_plane(d)
+        )
+
+    for n, d in enumerate(order[1:-1]):
+        if n == planes // 4:
+            z_rows[0] = chosen_rows(0, 2, Z_SLOTS)
+        if n == len(order) - 4:
+            send_rows(far_plane, 4, FAR_SLOTS)
+        send_rows(d, 2, Z_SLOTS)
+    far_rows[...] = chosen_rows(far_plane, 3, owners_in * NEAR_SLOTS)
+    last_copies = []
+    for k in range(owners_in):
+        start = pl.multiple_of(at_col(k) * NEAR_SLOTS, NEAR_SLOTS)
+        last_copies.append(
+            send(
+                far_rows.at[pl.ds(start, NEAR_SLOTS)],
+                last_rows.at[pl.ds(k * SLOTS, NEAR_SLOTS)],
+                far_send.at[k],
+                far_recv.at[k],
+                to_far(k),
             )
+        )
 
     for copy in lid_copies:
         copy.wait_recv()
@@ -221,20 +263,23 @@
         for k in range(1, owners_in)
     ]
     before = hot(iota((lanes, lanes), 0) < iota((lanes, lanes), 1))
-    rank = dot(hot(lids > 0.0), before)
-    source = jnp.where(lids > 0.0, rank, -1.0)
+    near_slot = lax.rem(iota((planes, lanes), 1), SLOTS) < NEAR_SLOTS
+    last = near_slot & (iota((planes, lanes), 0) == far_plane)
+    taken = (lids > 0.0) & jnp.logical_not(last)
+    source = jnp.where(taken, dot(hot(taken), before), -1.0)
     source = jnp.concatenate([source, jnp.zeros((BLOCK - planes, lanes), F32)], axis=0).T
 
     def forward_rows(d):
         if d:
             row_copies[d].wait_recv()
-        take = source[:, d : d + 1].astype(jnp.int32) == iota((lanes, Z_SLOTS), 1)
-        staged[d] = dot(hot(take), z_rows[d]).astype(BF16)
+        count, skip = (FAR_SLOTS, NEAR_SLOTS) if d == far_plane else (Z_SLOTS, 0)
+        take = source[:, d : d + 1].astype(jnp.int32) == iota((lanes, count), 1)
+        staged[d] = dot(hot(take), z_rows[d, :count, :]).astype(BF16)
         copies = []
         for k in range(owners_in):
-            start = pl.multiple_of(at_col(k) * SLOTS, SLOTS)
-            src = staged.at[d, pl.ds(start, SLOTS)]
-            dst = rows.at[d, pl.ds(k * SLOTS, SLOTS)]
+            start = pl.multiple_of(at_col(k) * SLOTS + skip, NEAR_SLOTS)
+            src = staged.at[d, pl.ds(start, SLOTS - skip)]
+            dst = rows.at[d, pl.ds(k * SLOTS + skip, SLOTS - skip)]
             if k == 0:
                 copy = pltpu.make_async_copy(src, dst, x_recv.at[d, 0])
                 copy.start()
@@ -243,7 +288,8 @@
             copies.append(copy)
         return copies
 
-    x_copies = {order[0]: forward_rows(order[0])}
+    steps = order[:-LATE] + [far_plane] + order[-LATE:-1]
+    x_copies = {steps[0]: forward_rows(steps[0])}
 
     for copy in col_lid_copies:
         copy.wait_recv()
@@ -257,19 +303,24 @@
 
     def set_of(d):
         which = jnp.zeros(d.shape, jnp.int32)
-        for n in range(LATE):
-            which = jnp.where(d == order[first_late + n], n + 1, which)
+        for n in range(1, LATE):
+            which = jnp.where(d == order[n - LATE - 1 + planes], n, which)
         return which
 
-    member = jnp.concatenate([hot(got == c + 1.0) for c in range(CLU_OWN)], axis=0)
+    other = jnp.where(last, 0.0, got)
+    member = jnp.concatenate([hot(other == c + 1.0) for c in range(CLU_OWN)], axis=0)
+    ending = jnp.where(near_slot, got, 0.0)[far_plane : far_plane + 1]
+    ending = hot(ending == iota((CLU_OWN, lanes), 0).astype(F32) + 1.0)
+    ending_rank = dot(ending, before)
+    ending_size = dot(ending, jnp.ones((lanes, lanes), BF16))
     in_row = dot(member, before)
     in_rows = dot(member, jnp.ones((lanes, lanes), BF16)).astype(BF16)
     a, b = (iota((CLU_OWN * planes, CLU_OWN * planes), n) for n in (0, 1))
     same = (a // planes == b // planes) & (set_of(lax.rem(a, planes)) == set_of(lax.rem(b, planes)))
     rank_all = in_row + dot(hot(same & (b < a)), in_rows)
-    a, b = (iota((CLU_OWN * (LATE + 1), CLU_OWN * planes), n) for n in (0, 1))
+    a, b = (iota((CLU_OWN * LATE, CLU_OWN * planes), n) for n in (0, 1))
     same = (lax.rem(a, CLU_OWN) == b // planes) & (a // CLU_OWN == set_of(lax.rem(b, planes)))
-    sizes = dot(hot(same), in_rows)
+    sizes = jnp.concatenate([dot(hot(same), in_rows), ending_size], axis=0)
     unfit = (
         (most(marks) >= TOO_MANY)
         | (most(sizes[:CLU_OWN]) > MANY)
@@ -278,24 +329,27 @@
     ranked = jnp.zeros((planes, lanes), F32)
     for c in range(CLU_OWN):
         this = slice(c * planes, (c + 1) * planes)
-        ranked += jnp.where(got == c + 1.0, rank_all[this], 0.0)
-    late = set_of(iota((planes, lanes), 0))
+        rank_here = jnp.where(last, ending_rank[c : c + 1], rank_all[this])
+        ranked += jnp.where(got == c + 1.0, rank_here, 0.0)
+    late = jnp.where(last, LATE, set_of(iota((planes, lanes), 0)))
     cluster = got.astype(jnp.int32) - 1
     ranked = ranked.astype(jnp.int32)
     target = jnp.where(cluster >= 0, cluster * jnp.where(late == 0, MANY, FEW) + ranked, -1)
 
+    def place_few(n, goal, arrived):
+        moved = dot(hot(iota((CLU_OWN * FEW, lanes), 0) == goal), arrived).astype(BF16)
+        for c in range(CLU_OWN):
+            sorted_rows[c, STARTS[n] : STARTS[n] + FEW, :] = moved[c * FEW : (c + 1) * FEW]
+
     def place_rows(n):
-        d = order[n]
+        d = steps[n]
         copies = x_copies[d]
         copies[0].wait()
         for copy in copies[1:]:
             copy.wait_recv()
-        goal = target[d : d + 1]
+        goal = jnp.where(last, -1, target)[d : d + 1]
         if n >= first_late:
-            moved = dot(hot(iota((CLU_OWN * FEW, lanes), 0) == goal), rows[d]).astype(BF16)
-            start = STARTS[n - first_late + 1]
-            for c in range(CLU_OWN):
-                sorted_rows[c, start : start + FEW, :] = moved[c * FEW : (c + 1) * FEW]
+            place_few(n - first_late + 1, goal, rows[d])
             return
 
         def body(c, carry):
@@ -438,22 +492,26 @@
             news.append(highest(total[full * BLOCK :], limit))
         by_new[s] = functools.reduce(jnp.maximum, news)
 
-    for n in range(planes):
-        if n:
-            x_copies[order[n]] = forward_rows(order[n])
-            place_rows(n - 1)
-            s = n - first_late
-            if s == 0:
-                begin_sum(0)
-            elif s > 0:
-                relay_sum(s - 1)
-                begin_sum(s)
-                if s >= 2:
-                    best_of(s - 2)
+    def after(n):
+        s = n - first_late + 1
+        if s == 0:
+            begin_sum(0)
+        elif s > 0:
+            relay_sum(s - 1)
+            begin_sum(s)
+            if s >= 2:
+                best_of(s - 2)
+
+    for n in range(1, planes):
+        x_copies[steps[n]] = forward_rows(steps[n])
+        place_rows(n - 1)
+        after(n - 1)
     place_rows(planes - 1)
-    relay_sum(LATE - 1)
-    begin_sum(LATE)
-    best_of(LATE - 2)
+    after(planes - 1)
+    for copy in last_copies:
+        copy.wait_recv()
+    place_few(LATE, jnp.where(last, target, -1)[far_plane : far_plane + 1], last_rows[...])
+    after(planes)
     relay_sum(LATE)
     best_of(LATE - 1)
     best_of(LATE)
@@ -480,10 +538,24 @@
             values = jnp.where(where_row[d : d + 1] == n, table[:, n : n + 1], values)
         mask = iota((BLOCK, lanes), 0) == where_lane[d : d + 1]
         picked.append(jnp.sum(jnp.where(mask, values, 0.0), axis=0, keepdims=True))
-    values_out[...] = jnp.where(unfit, TOO_MANY, jnp.concatenate(picked, axis=0))
+    values = jnp.where(unfit, TOO_MANY, jnp.concatenate(picked, axis=0))
+
+    def turn(v):
+        shifted = [v] + [pltpu.roll(v, n * SLOTS, 1) for n in range(1, planes)]
+        mine = iota(v.shape, 0) == group
+        lines = []
+        for b in range(planes):
+            line = jnp.zeros(v.shape, F32)
+            for a in range(planes):
+                line = jnp.where(mine & (group == a), shifted[(a - b) % planes], line)
+            lines.append(jnp.sum(line, axis=0, keepdims=True))
+        return lines
+
+    for k, line in enumerate(turn(values)):
+        values_out[k] = line
     col_back = [
         send(
-            values_out,
+            values_out.at[k],
             x_back.at[j, k],
             xb_send.at[j, k],
             xb_recv.at[j, k],
@@ -493,30 +565,30 @@
         for j in range(4)
         if k or j
     ]
-    home = jnp.where(group == 0, values_out[...], 0.0)
     for copy in col_back:
         copy.wait_recv()
+    home = []
     for k in range(owners_in):
-        for j in range(4):
-            if k or j:
-                home += jnp.where(group == k, x_back[j, k], 0.0)
-    values_home[...] = pltpu.roll(home, my_col * SLOTS, 1)
+        parts = [x_back[j, k] if k or j else values_out[0] for j in range(4)]
+        home.append(functools.reduce(jnp.add, parts))
+    home = jnp.concatenate(turn(jnp.concatenate(home, axis=0)), axis=0)
+    home = pltpu.roll(home, my_col * SLOTS, 1)
+    for d in range(planes):
+        values_home[d] = home[d : d + 1]
     plane_back = [
-        send(values_home, z_back.at[d], zb_send.at[d], zb_recv.at[d], to_plane(planes - d))
+        send(
+            values_home.at[d], z_back.at[d], zb_send.at[d], zb_recv.at[d], to_plane(planes - d)
+        )
         for d in range(1, planes)
     ]
     for copy in plane_back:
         copy.wait_recv()
-    marks = values_home[...]
-    for d in range(1, planes):
-        marks = jnp.maximum(marks, z_back[d])
-    flag_ref[0, 0] = jnp.max(marks)
-    mine = jnp.concatenate(
-        [values_home[0:1]] + [z_back[d][d : d + 1] for d in range(1, planes)], axis=0
-    )
+    mine = jnp.concatenate([values_home[0]] + [z_back[d] for d in range(1, planes)], axis=0)
+    flag_ref[0, 0] = jnp.max(mine)
     mine = jnp.concatenate([mine, jnp.zeros((BLOCK - planes, lanes), F32)], axis=0).T
-    chosen = jnp.where(iota((BLOCK, items), 0) == index[0:1, :], 1.0, 0.0)
-    values = dot(mine, chosen, precision=lax.Precision.HIGHEST)
+    values = jnp.zeros((lanes, items), F32)
+    for d in range(planes):
+        values = jnp.where(index[0:1, :] == d, mine[:, d : d + 1], values)
     mask = iota((lanes, items), 0) == index[1:2, :]
     out_ref[...] = jnp.sum(jnp.where(mask, values, 0.0), axis=0, keepdims=True)
 
@@ -548,16 +620,18 @@
             buffer((owners_in, planes, lanes), F32),
             buffer((planes, lanes, part), BF16),
             buffer((planes, lanes, part), BF16),
+            buffer((owners_in * NEAR_SLOTS, part), BF16),
+            buffer((lanes, part), BF16),
             buffer((CLU_OWN, CAP, part), BF16),
             buffer((4, total, BLOCK), F32),
             buffer((2, total // 2, BLOCK), F32),
             buffer((2, total // 2, BLOCK), F32),
             buffer((2, total // 2, BLOCK), F32),
             buffer((2, total // 2, BLOCK), F32),
-            buffer((planes, lanes), F32),
-            buffer((4, owners_in, planes, lanes), F32),
-            buffer((planes, lanes), F32),
-            buffer((planes, planes, lanes), F32),
+            buffer((owners_in, 1, lanes), F32),
+            buffer((4, owners_in, 1, lanes), F32),
+            buffer((planes, 1, lanes), F32),
+            buffer((planes, 1, lanes), F32),
             dma(items // BLOCK),
             dma(planes),
             dma(planes),
@@ -567,6 +641,8 @@
             dma(owners_in),
             dma(planes, owners_in),
             dma(planes, owners_in),
+            dma(owners_in),
+            dma(owners_in),
             dma(LATE + 1, 6),
             dma(LATE + 1, 6),
             dma(4, owners_in),

time: 126 us -> 121 us (0.960)
  Pallas kernels: 125 us -> 119 us
    pallas_call x1, Pallas kernels: 125 us -> 119 us  [fast(): pl.pallas_call(functools.partial(kernel, planes, owners_in), out_shape=(j...]
where the time goes in v4:
time: 121 us
  Pallas kernels  119 us (98%)
    pallas_call x1, Pallas kernels, fast(): pl.pallas_call(functools.partial(kernel, planes, owners_in), out_shape=(j...  119 us

profile of v4, /device:TPU:1, one launch (start us, length us, event | category | flops | bytes accessed | tf_op | source)
XLA Modules:
  0.0 120.8 jit_solution(13964192032604670703)
XLA Ops:
  0.0 119.2 %shard_map.30 = (f32[1,1024]{1,0:T(1,128)S(1)}, f32[1,1]{1,0:T(1,128)}) custom-call(s32[1,1024]{1,0:T(1,128)} %bitcast.27, bf16[1024,4096]{1,0:T(8,128)(2,1)} %x_ref.1), custom_call_target="tpu_custom_call" | custom-call | tf_op jit(solution)/shard_map/pallas_call | solution.py:606
  119.9 0.3 conditional.1
  120.2 0.6 copy.16

commit v5 on v4

--- a/solution.py
+++ b/solution.py
@@ -15,10 +15,12 @@
 BLOCK = 128
 LATE = 3
 FEW = 64
+LAST = 48
 MANY = 2 * BLOCK
 CAP = MANY + LATE * FEW
 STARTS = (0, MANY, MANY + FEW, MANY + 2 * FEW)
-SCORE_ROWS = (4 * BLOCK, 2 * BLOCK + FEW, 3 * BLOCK, 3 * BLOCK + FEW)
+NEW = (0, FEW, FEW, LAST)
+SCORE_ROWS = (4 * BLOCK, 5 * FEW, 6 * FEW, 7 * LAST)
 TOO_MANY = 4.0 * CLU_OWN
 F32 = jnp.float32
 BF16 = jnp.bfloat16
@@ -155,13 +157,9 @@
     for d in range(1, planes):
         pl.semaphore_signal(barrier, inc=1, device_id=to_plane(d), device_id_type=MESH)
     for k in range(1, owners_in):
-        pl.semaphore_signal(barrier, inc=1, device_id=to_far(k), device_id_type=MESH)
-    for k in range(owners_in):
-        for j in range(4):
-            if k or j:
-                pl.semaphore_signal(
-                    barrier, inc=1, device_id=to_both(k, j), device_id_type=MESH
-                )
+        pl.semaphore_signal(barrier, inc=1, device_id=to_col(k), device_id_type=MESH)
+    for k in range(1, 4):
+        pl.semaphore_signal(barrier, inc=1, device_id=to_tile(k), device_id_type=MESH)
 
     ids = ids_ref[...]
     owner = ids // CLU_OWN
@@ -214,7 +212,7 @@
 
     lax.fori_loop(0, blocks, unit_rows, 0)
 
-    pl.semaphore_wait(barrier, planes - 1 + owners_in - 1 + 4 * owners_in - 1)
+    pl.semaphore_wait(barrier, planes - 1 + owners_in - 1 + 3)
     lid_copies = [
         send(lids_own.at[at_plane(d)], z_lids.at[d], zl_send.at[d], zl_recv.at[d], to_plane(d))
         for d in order[1:]
@@ -225,32 +223,47 @@
         wanted = jnp.where(index[0:1, :] == d, index[line : line + 1, :], -1)
         return dot(hot(iota((count, items), 0) == wanted), unit[...]).astype(BF16)
 
-    def send_rows(d, line, count):
+    def pack_rows(d, line, count):
         packed[d, :count, :] = chosen_rows(d, line, count)
+
+    def send_rows(d, count):
         at = pl.ds(0, count)
         row_copies[d] = send(
             packed.at[d, at], z_rows.at[d, at], z_send.at[d], z_recv.at[d], to_plane(d)
         )
 
-    for n, d in enumerate(order[1:-1]):
-        if n == planes // 4:
+    held = order[-LATE:-1]
+    for n, d in enumerate(order[1:-LATE]):
+        pack_rows(d, 2, Z_SLOTS)
+        send_rows(d, Z_SLOTS)
+        if n == 1:
             z_rows[0] = chosen_rows(0, 2, Z_SLOTS)
-        if n == len(order) - 4:
-            send_rows(far_plane, 4, FAR_SLOTS)
-        send_rows(d, 2, Z_SLOTS)
+    if planes < 8:
+        z_rows[0] = chosen_rows(0, 2, Z_SLOTS)
+    pack_rows(far_plane, 4, FAR_SLOTS)
+    send_rows(far_plane, FAR_SLOTS)
+    for d in held:
+        pack_rows(d, 2, Z_SLOTS)
     far_rows[...] = chosen_rows(far_plane, 3, owners_in * NEAR_SLOTS)
+
+    def send_held():
+        for d in held:
+            send_rows(d, Z_SLOTS)
+
     last_copies = []
-    for k in range(owners_in):
-        start = pl.multiple_of(at_col(k) * NEAR_SLOTS, NEAR_SLOTS)
-        last_copies.append(
-            send(
-                far_rows.at[pl.ds(start, NEAR_SLOTS)],
-                last_rows.at[pl.ds(k * SLOTS, NEAR_SLOTS)],
-                far_send.at[k],
-                far_recv.at[k],
-                to_far(k),
+
+    def send_last():
+        for k in range(owners_in):
+            start = pl.multiple_of(at_col(k) * NEAR_SLOTS, NEAR_SLOTS)
+            last_copies.append(
+                send(
+                    far_rows.at[pl.ds(start, NEAR_SLOTS)],
+                    last_rows.at[pl.ds(k * SLOTS, NEAR_SLOTS)],
+                    far_send.at[k],
+                    far_recv.at[k],
+                    to_far(k),
+                )
             )
-        )
 
     for copy in lid_copies:
         copy.wait_recv()
@@ -325,6 +338,7 @@
         (most(marks) >= TOO_MANY)
         | (most(sizes[:CLU_OWN]) > MANY)
         | (most(sizes[CLU_OWN:]) > FEW)
+        | (most(sizes[CLU_OWN * LATE :]) > LAST)
     )
     ranked = jnp.zeros((planes, lanes), F32)
     for c in range(CLU_OWN):
@@ -381,21 +395,21 @@
                     c > r, all_pairs[:BLOCK, :BLOCK], all_pairs[BLOCK:, BLOCK:]
                 )
             return
-        start, stop = STARTS[s], STARTS[s] + FEW
+        start, stop, fresh = STARTS[s], STARTS[s] + FEW, NEW[s]
         full = stop // BLOCK
         ends = []
         for j in range(2):
-            new = sorted_rows[2 * t + j, start:stop, :]
+            new = sorted_rows[2 * t + j, start : start + fresh, :]
             pairs = dot(new, sorted_rows[2 * t + j, : full * BLOCK, :], NT)
             for p in range(full):
-                at = base + p * BLOCK + j * FEW
-                partial[t, at : at + FEW] = pairs[:, p * BLOCK : (p + 1) * BLOCK]
+                at = base + (2 * p + j) * fresh
+                partial[t, at : at + fresh] = pairs[:, p * BLOCK : (p + 1) * BLOCK]
             if stop % BLOCK:
                 ends.append(dot(new, sorted_rows[2 * t + j, start - FEW : stop, :], NT))
         if ends:
-            at = base + full * BLOCK
-            partial[t, at : at + FEW] = jnp.where(
-                c[:FEW] < FEW, pltpu.roll(ends[0], FEW, 1), ends[1]
+            at = base + 2 * full * fresh
+            partial[t, at : at + fresh] = jnp.where(
+                c[:fresh] < FEW, pltpu.roll(ends[0], FEW, 1), ends[1]
             )
 
     y_copies = {}
@@ -469,49 +483,54 @@
                 raise_to(j, 1, highest(turned, high & above))
                 raise_to(j, 1, highest(cross, low))
             return
-        start, stop = STARTS[s], STARTS[s] + FEW
+        stop, fresh = STARTS[s] + FEW, NEW[s]
         full = stop // BLOCK
-        row_few, col_few = r[:FEW], c[:FEW]
+        row_few, col_few = r[:fresh], c[:fresh]
         news = []
         for p in range(full):
-            tile_p = total[p * BLOCK : (p + 1) * BLOCK]
+            halves = [total[(2 * p + j) * fresh : (2 * p + j + 1) * fresh] for j in range(2)]
             for j in range(2):
                 limit = row_few < size[s][j]
                 if (p + 1) * BLOCK == stop:
                     limit = limit & (col_few - FEW != row_few)
-                raise_to(j, p, highest(tile_p[j * FEW : (j + 1) * FEW], limit))
+                raise_to(j, p, highest(halves[j], limit))
             if p < 2:
                 earlier = r + p * BLOCK < size_both[0]
             else:
                 earlier = (r < FEW) & (r < size_both[1])
                 if s == 3:
                     earlier = earlier | ((r >= FEW) & (r - FEW < size_both[2]))
-            news.append(highest(tile_p.T, earlier))
+            if fresh < FEW:
+                blank = jnp.zeros((FEW - fresh, BLOCK), F32)
+                halves = [halves[0], blank, halves[1], blank]
+            news.append(highest(jnp.concatenate(halves, axis=0).T, earlier))
         if stop % BLOCK:
             limit = (row_few < size_both[s]) & (row_few != lax.rem(col_few, FEW))
-            news.append(highest(total[full * BLOCK :], limit))
+            news.append(highest(total[2 * full * fresh :], limit))
         by_new[s] = functools.reduce(jnp.maximum, news)
-
-    def after(n):
-        s = n - first_late + 1
-        if s == 0:
-            begin_sum(0)
-        elif s > 0:
-            relay_sum(s - 1)
-            begin_sum(s)
-            if s >= 2:
-                best_of(s - 2)
 
     for n in range(1, planes):
         x_copies[steps[n]] = forward_rows(steps[n])
+        if n == planes // 4:
+            send_held()
+        if n == planes - 2:
+            send_last()
         place_rows(n - 1)
-        after(n - 1)
+        if n == first_late:
+            begin_sum(0)
+        elif n > first_late:
+            begin_sum(n - first_late)
+            relay_sum(n - first_late - 1)
     place_rows(planes - 1)
-    after(planes - 1)
+    begin_sum(LATE - 1)
+    relay_sum(LATE - 2)
+    best_of(0)
     for copy in last_copies:
         copy.wait_recv()
     place_few(LATE, jnp.where(last, target, -1)[far_plane : far_plane + 1], last_rows[...])
-    after(planes)
+    begin_sum(LATE)
+    relay_sum(LATE - 1)
+    best_of(LATE - 2)
     relay_sum(LATE)
     best_of(LATE - 1)
     best_of(LATE)

time: 121 us -> 114 us (0.942)
  Pallas kernels: 119 us -> 113 us
    pallas_call x1, Pallas kernels: 119 us -> 113 us  [fast(): pl.pallas_call(functools.partial(kernel, planes, owners_in), out_shape=(j...]
where the time goes in v5:
time: 114 us
  Pallas kernels  113 us (99%)
    pallas_call x1, Pallas kernels, fast(): pl.pallas_call(functools.partial(kernel, planes, owners_in), out_shape=(j...  113 us

profile of v5, /device:TPU:1, one launch (start us, length us, event | category | flops | bytes accessed | tf_op | source)
XLA Modules:
  0.0 114.3 jit_solution(10722779554702739748)
XLA Ops:
  0.0 112.7 %shard_map.30 = (f32[1,1024]{1,0:T(1,128)S(1)}, f32[1,1]{1,0:T(1,128)}) custom-call(s32[1,1024]{1,0:T(1,128)} %bitcast.27, bf16[1024,4096]{1,0:T(8,128)(2,1)} %x_ref.1), custom_call_target="tpu_custom_call" | custom-call | tf_op jit(solution)/shard_map/pallas_call | solution.py:625
  113.4 0.3 conditional.1
  113.7 0.6 copy.16

commit v6 on v5

--- a/solution.py
+++ b/solution.py
@@ -126,7 +126,10 @@
     first_late = planes - LATE + 1
     started = []
 
-    def send(src, dst, send_sem, recv_sem, device):
+    def drain(ref, sem):
+        pltpu.make_async_copy(ref, ref, sem).wait()
+
+    def send(src, dst, send_sem, recv_sem, device, alone=False):
         copy = pltpu.make_async_remote_copy(
             src_ref=src,
             dst_ref=dst,
@@ -136,8 +139,17 @@
             device_id_type=MESH,
         )
         copy.start()
-        started.append(copy)
+        if alone:
+            started.append(copy)
         return copy
+
+    barrier = pltpu.get_barrier_semaphore()
+    for d in range(1, planes):
+        pl.semaphore_signal(barrier, inc=1, device_id=to_plane(d), device_id_type=MESH)
+    for k in range(1, owners_in):
+        pl.semaphore_signal(barrier, inc=1, device_id=to_col(k), device_id_type=MESH)
+    for k in range(1, 4):
+        pl.semaphore_signal(barrier, inc=1, device_id=to_tile(k), device_id_type=MESH)
 
     loads = [
         pltpu.make_async_copy(
@@ -152,14 +164,6 @@
         blank = jnp.zeros((NEAR_SLOTS, part), BF16)
         rows[far_plane, k * SLOTS : k * SLOTS + NEAR_SLOTS, :] = blank
         last_rows[k * SLOTS + NEAR_SLOTS : (k + 1) * SLOTS, :] = blank
-
-    barrier = pltpu.get_barrier_semaphore()
-    for d in range(1, planes):
-        pl.semaphore_signal(barrier, inc=1, device_id=to_plane(d), device_id_type=MESH)
-    for k in range(1, owners_in):
-        pl.semaphore_signal(barrier, inc=1, device_id=to_col(k), device_id_type=MESH)
-    for k in range(1, 4):
-        pl.semaphore_signal(barrier, inc=1, device_id=to_tile(k), device_id_type=MESH)
 
     ids = ids_ref[...]
     owner = ids // CLU_OWN
@@ -213,10 +217,8 @@
     lax.fori_loop(0, blocks, unit_rows, 0)
 
     pl.semaphore_wait(barrier, planes - 1 + owners_in - 1 + 3)
-    lid_copies = [
-        send(lids_own.at[at_plane(d)], z_lids.at[d], zl_send.at[d], zl_recv.at[d], to_plane(d))
-        for d in order[1:]
-    ]
+    for d in order[1:]:
+        send(lids_own.at[at_plane(d)], z_lids.at[d], zl_send, zl_recv, to_plane(d))
     row_copies = {}
 
     def chosen_rows(d, line, count):
@@ -229,7 +231,7 @@
     def send_rows(d, count):
         at = pl.ds(0, count)
         row_copies[d] = send(
-            packed.at[d, at], z_rows.at[d, at], z_send.at[d], z_recv.at[d], to_plane(d)
+            packed.at[d, at], z_rows.at[d, at], z_send.at[d], z_recv.at[d], to_plane(d), True
         )
 
     held = order[-LATE:-1]
@@ -250,31 +252,24 @@
         for d in held:
             send_rows(d, Z_SLOTS)
 
-    last_copies = []
-
     def send_last():
         for k in range(owners_in):
             start = pl.multiple_of(at_col(k) * NEAR_SLOTS, NEAR_SLOTS)
-            last_copies.append(
-                send(
-                    far_rows.at[pl.ds(start, NEAR_SLOTS)],
-                    last_rows.at[pl.ds(k * SLOTS, NEAR_SLOTS)],
-                    far_send.at[k],
-                    far_recv.at[k],
-                    to_far(k),
-                )
+            send(
+                far_rows.at[pl.ds(start, NEAR_SLOTS)],
+                last_rows.at[pl.ds(k * SLOTS, NEAR_SLOTS)],
+                far_send,
+                far_recv,
+                to_far(k),
             )
 
-    for copy in lid_copies:
-        copy.wait_recv()
+    drain(z_lids.at[pl.ds(1, planes - 1)], zl_recv)
     lids = jnp.concatenate(
         [lids_own[my_plane][0:1]] + [z_lids[d][0:1] for d in range(1, planes)], axis=0
     )
     lids_out[...] = pltpu.roll(lids, lax.rem(owners_in - my_col, owners_in) * SLOTS, 1)
-    col_lid_copies = [
-        send(lids_out, x_lids.at[k], xl_send.at[k], xl_recv.at[k], to_col(k))
-        for k in range(1, owners_in)
-    ]
+    for k in range(1, owners_in):
+        send(lids_out, x_lids.at[k], xl_send, xl_recv, to_col(k))
     before = hot(iota((lanes, lanes), 0) < iota((lanes, lanes), 1))
     near_slot = lax.rem(iota((planes, lanes), 1), SLOTS) < NEAR_SLOTS
     last = near_slot & (iota((planes, lanes), 0) == far_plane)
@@ -282,30 +277,28 @@
     source = jnp.where(taken, dot(hot(taken), before), -1.0)
     source = jnp.concatenate([source, jnp.zeros((BLOCK - planes, lanes), F32)], axis=0).T
 
+    def others(d):
+        return pl.ds(0, (owners_in - 1) * (NEAR_SLOTS if d == far_plane else SLOTS))
+
     def forward_rows(d):
         if d:
             row_copies[d].wait_recv()
         count, skip = (FAR_SLOTS, NEAR_SLOTS) if d == far_plane else (Z_SLOTS, 0)
         take = source[:, d : d + 1].astype(jnp.int32) == iota((lanes, count), 1)
         staged[d] = dot(hot(take), z_rows[d, :count, :]).astype(BF16)
-        copies = []
         for k in range(owners_in):
             start = pl.multiple_of(at_col(k) * SLOTS + skip, NEAR_SLOTS)
             src = staged.at[d, pl.ds(start, SLOTS - skip)]
             dst = rows.at[d, pl.ds(k * SLOTS + skip, SLOTS - skip)]
-            if k == 0:
-                copy = pltpu.make_async_copy(src, dst, x_recv.at[d, 0])
-                copy.start()
+            if k:
+                send(src, dst, x_send.at[d], x_recv.at[d], to_col(k))
             else:
-                copy = send(src, dst, x_send.at[d, k], x_recv.at[d, k], to_col(k))
-            copies.append(copy)
-        return copies
+                rows[d, skip:SLOTS, :] = staged[d, pl.ds(start, SLOTS - skip), :]
 
     steps = order[:-LATE] + [far_plane] + order[-LATE:-1]
-    x_copies = {steps[0]: forward_rows(steps[0])}
-
-    for copy in col_lid_copies:
-        copy.wait_recv()
+    forward_rows(steps[0])
+
+    drain(x_lids.at[pl.ds(1, owners_in - 1)], xl_recv)
     got = jnp.zeros((planes, lanes), F32)
     marks = lids_out[...]
     group = iota((planes, lanes), 1) // SLOTS
@@ -357,10 +350,7 @@
 
     def place_rows(n):
         d = steps[n]
-        copies = x_copies[d]
-        copies[0].wait()
-        for copy in copies[1:]:
-            copy.wait_recv()
+        drain(rows.at[d, others(d)], x_recv.at[d])
         goal = jnp.where(last, -1, target)[d : d + 1]
         if n >= first_late:
             place_few(n - first_late + 1, goal, rows[d])
@@ -415,7 +405,7 @@
     y_copies = {}
 
     def y_send_to(s, n, src, dst, step):
-        y_copies[s, n] = send(src, dst, y_send.at[s, n], y_recv.at[s, n], to_tile(step))
+        y_copies[s, n] = send(src, dst, y_send, y_recv.at[s, n], to_tile(step))
 
     def begin_sum(s):
         base, half = spans[s]
@@ -510,7 +500,7 @@
         by_new[s] = functools.reduce(jnp.maximum, news)
 
     for n in range(1, planes):
-        x_copies[steps[n]] = forward_rows(steps[n])
+        forward_rows(steps[n])
         if n == planes // 4:
             send_held()
         if n == planes - 2:
@@ -525,8 +515,7 @@
     begin_sum(LATE - 1)
     relay_sum(LATE - 2)
     best_of(0)
-    for copy in last_copies:
-        copy.wait_recv()
+    drain(last_rows.at[pl.ds(0, owners_in * NEAR_SLOTS)], far_recv)
     place_few(LATE, jnp.where(last, target, -1)[far_plane : far_plane + 1], last_rows[...])
     begin_sum(LATE)
     relay_sum(LATE - 1)
@@ -572,36 +561,23 @@
 
     for k, line in enumerate(turn(values)):
         values_out[k] = line
-    col_back = [
-        send(
-            values_out.at[k],
-            x_back.at[j, k],
-            xb_send.at[j, k],
-            xb_recv.at[j, k],
-            to_both(owners_in - k, j),
-        )
-        for k in range(owners_in)
-        for j in range(4)
-        if k or j
-    ]
-    for copy in col_back:
-        copy.wait_recv()
+    for k in range(owners_in):
+        for j in range(4):
+            if k or j:
+                dst = x_back.at[j * owners_in + k]
+                send(values_out.at[k], dst, xb_send, xb_recv, to_both(owners_in - k, j))
+    drain(x_back.at[pl.ds(1, 4 * owners_in - 1)], xb_recv)
     home = []
     for k in range(owners_in):
-        parts = [x_back[j, k] if k or j else values_out[0] for j in range(4)]
+        parts = [x_back[j * owners_in + k] if k or j else values_out[0] for j in range(4)]
         home.append(functools.reduce(jnp.add, parts))
     home = jnp.concatenate(turn(jnp.concatenate(home, axis=0)), axis=0)
     home = pltpu.roll(home, my_col * SLOTS, 1)
     for d in range(planes):
         values_home[d] = home[d : d + 1]
-    plane_back = [
-        send(
-            values_home.at[d], z_back.at[d], zb_send.at[d], zb_recv.at[d], to_plane(planes - d)
-        )
-        for d in range(1, planes)
-    ]
-    for copy in plane_back:
-        copy.wait_recv()
+    for d in range(1, planes):
+        send(values_home.at[d], z_back.at[d], zb_send, zb_recv, to_plane(planes - d))
+    drain(z_back.at[pl.ds(1, planes - 1)], zb_recv)
     mine = jnp.concatenate([values_home[0]] + [z_back[d] for d in range(1, planes)], axis=0)
     flag_ref[0, 0] = jnp.max(mine)
     mine = jnp.concatenate([mine, jnp.zeros((BLOCK - planes, lanes), F32)], axis=0).T
@@ -613,6 +589,14 @@
 
     for copy in started:
         copy.wait_send()
+    for d in order:
+        drain(staged.at[d, others(d)], x_send.at[d])
+    drain(far_rows, far_send)
+    drain(partial.at[pl.ds(0, 3)], y_send)
+    drain(z_lids.at[pl.ds(1, planes - 1)], zl_send)
+    drain(x_lids.at[pl.ds(1, owners_in - 1)], xl_send)
+    drain(x_back.at[pl.ds(1, 4 * owners_in - 1)], xb_send)
+    drain(z_back.at[pl.ds(1, planes - 1)], zb_send)
 
 
 def fast(planes, owners_in, embeddings, cluster_ids, part):
@@ -620,7 +604,8 @@
     lanes = owners_in * SLOTS
     total = sum(SCORE_ROWS)
     vmem = pl.BlockSpec(memory_space=pltpu.VMEM)
-    dma = lambda *shape: pltpu.SemaphoreType.DMA(shape)
+    one = pltpu.SemaphoreType.DMA
+    dma = lambda *shape: one(shape)
     buffer = pltpu.VMEM
     return pl.pallas_call(
         functools.partial(kernel, planes, owners_in),
@@ -648,26 +633,26 @@
             buffer((2, total // 2, BLOCK), F32),
             buffer((2, total // 2, BLOCK), F32),
             buffer((owners_in, 1, lanes), F32),
-            buffer((4, owners_in, 1, lanes), F32),
+            buffer((4 * owners_in, 1, lanes), F32),
             buffer((planes, 1, lanes), F32),
             buffer((planes, 1, lanes), F32),
             dma(items // BLOCK),
             dma(planes),
             dma(planes),
+            one,
+            one,
+            one,
+            one,
             dma(planes),
             dma(planes),
-            dma(owners_in),
-            dma(owners_in),
-            dma(planes, owners_in),
-            dma(planes, owners_in),
-            dma(owners_in),
-            dma(owners_in),
+            one,
+            one,
+            one,
             dma(LATE + 1, 6),
-            dma(LATE + 1, 6),
-            dma(4, owners_in),
-            dma(4, owners_in),
-            dma(planes),
-            dma(planes),
+            one,
+            one,
+            one,
+            one,
         ],
         compiler_params=pltpu.CompilerParams(
             collective_id=0, has_side_effects=True, vmem_limit_bytes=60 * 1024 * 1024

time: 114 us -> 112 us (0.982)
  Pallas kernels: 113 us -> 110 us
    pallas_call x1, Pallas kernels: 113 us -> 110 us  [fast(): pl.pallas_call(functools.partial(kernel, planes, owners_in), out_shape=(j...]
where the time goes in v6:
time: 112 us
  Pallas kernels  110 us (98%)
    pallas_call x1, Pallas kernels, fast(): pl.pallas_call(functools.partial(kernel, planes, owners_in), out_shape=(j...  110 us

profile of v6, /device:TPU:1, one launch (start us, length us, event | category | flops | bytes accessed | tf_op | source)
XLA Modules:
  0.0 111.8 jit_solution(8967975756369658660)
XLA Ops:
  0.0 110.2 %shard_map.30 = (f32[1,1024]{1,0:T(1,128)S(1)}, f32[1,1]{1,0:T(1,128)}) custom-call(s32[1,1024]{1,0:T(1,128)} %bitcast.27, bf16[1024,4096]{1,0:T(8,128)(2,1)} %x_ref.1), custom_call_target="tpu_custom_call" | custom-call | tf_op jit(solution)/shard_map/pallas_call | solution.py:610
  110.9 0.3 conditional.1
  111.2 0.6 copy.16

commit v7 on v6

--- a/solution.py
+++ b/solution.py
@@ -500,17 +500,22 @@
         by_new[s] = functools.reduce(jnp.maximum, news)
 
     for n in range(1, planes):
+        if n == first_late:
+            place_rows(n - 1)
+            begin_sum(0)
         forward_rows(steps[n])
         if n == planes // 4:
             send_held()
         if n == planes - 2:
             send_last()
-        place_rows(n - 1)
         if n == first_late:
-            begin_sum(0)
-        elif n > first_late:
+            relay_sum(0)
+        else:
+            place_rows(n - 1)
+        if n > first_late:
             begin_sum(n - first_late)
-            relay_sum(n - first_late - 1)
+            if n > first_late + 1:
+                relay_sum(n - first_late - 1)
     place_rows(planes - 1)
     begin_sum(LATE - 1)
     relay_sum(LATE - 2)
@@ -561,8 +566,8 @@
 
     for k, line in enumerate(turn(values)):
         values_out[k] = line
-    for k in range(owners_in):
-        for j in range(4):
+    for k in reversed(nearest_first(owners_in)):
+        for j in (2, 1, 3, 0):
             if k or j:
                 dst = x_back.at[j * owners_in + k]
                 send(values_out.at[k], dst, xb_send, xb_recv, to_both(owners_in - k, j))
@@ -575,7 +580,7 @@
     home = pltpu.roll(home, my_col * SLOTS, 1)
     for d in range(planes):
         values_home[d] = home[d : d + 1]
-    for d in range(1, planes):
+    for d in reversed(order[1:]):
         send(values_home.at[d], z_back.at[d], zb_send, zb_recv, to_plane(planes - d))
     drain(z_back.at[pl.ds(1, planes - 1)], zb_recv)
     mine = jnp.concatenate([values_home[0]] + [z_back[d] for d in range(1, planes)], axis=0)

time: 112 us -> 112 us (level)
  no operation moved by 1% of the time
where the time goes in v7:
time: 112 us
  Pallas kernels  110 us (98%)
    pallas_call x1, Pallas kernels, fast(): pl.pallas_call(functools.partial(kernel, planes, owners_in), out_shape=(j...  110 us

profile of v7, /device:TPU:1, one launch (start us, length us, event | category | flops | bytes accessed | tf_op | source)
XLA Modules:
  0.0 112.0 jit_solution(15805781625306559802)
XLA Ops:
  0.0 110.4 %shard_map.30 = (f32[1,1024]{1,0:T(1,128)S(1)}, f32[1,1]{1,0:T(1,128)}) custom-call(s32[1,1024]{1,0:T(1,128)} %bitcast.27, bf16[1024,4096]{1,0:T(8,128)(2,1)} %x_ref.1), custom_call_target="tpu_custom_call" | custom-call | tf_op jit(solution)/shard_map/pallas_call | solution.py:615
  111.1 0.3 conditional.1
  111.4 0.6 copy.16
